TPU v7x, 512 devices: a whole 4x4x16 slice. The times are simulated.
512 devices in a mesh: ka: 16 (over z_lo, core), tau: 32 (over y, z_hi, x).
Axes of the slice: x: 4, y: 4, z: 16 (z_hi: 2, z_lo: 8; z = z_hi * 8 + z_lo), core: 2. Of those that a mesh axis runs over, the one named last changes fastest.
Arguments:
- bcoef: bfloat16 [16, 16, 384, 384], P('ka', None, 'tau'), may hold values from -0.3125 to 0.3125
- fwd_green: bfloat16 [16, 32, 384, 384], P('ka', 'tau'), may hold values from -0.3125 to 0.3125
- back_green: bfloat16 [16, 32, 384, 384], P('ka', 'tau'), may hold values from -0.3125 to 0.3125
- kmq: int32 [16], P('ka'), may hold values from 0 to 15, as said below
- ir_table: float32 [2, 128, 32], replicated, may hold values from -6 to 6
- ir_fit: float32 [32, 32], replicated, may hold values from -1 to 1
- freq_index: int32 [32], replicated, may hold values from 0 to 127
Outputs:
- polar_freq: float32 [2, 32, 16, 16], P(None, 'tau', 'ka')
Inputs may be any that keep to these rules, and one draw needn't show every extreme that they name: kmq[k] is the index of k - q on a 4 x 4 grid of k-points numbered row by row with wrap-around, for one q whose two components are both nonzero (each 1 to 3); it is a permutation.
All inputs are finite; a program needn't handle non-finite values.
Results may differ from a plain program's by a relative error of at most 0.004.
Values may be sent and summed in bfloat16 or wider, within the bound.
No kernel may reach another device: no remote copies, remote signals or barrier semaphores. Data moves between devices by JAX's collectives and lax.ppermute only.
A program may use at most 64 MiB of HBM per device.

v0:
```python
import functools

import jax
import jax.numpy as jnp
from jax import lax
from jax.experimental import pallas as pl
from jax.experimental.pallas import tpu as pltpu
from jax.sharding import Mesh
from jax.sharding import PartitionSpec as P

SIDE = 4
TILE = 16
POINTS = 16
VMEM_LIMIT = 24 * 1024 * 1024
SMALL_LIMIT = 8 * 1024 * 1024
COST = pl.CostEstimate(flops=1000, bytes_accessed=1000, transcendentals=0)


def onehot(rows, columns):
    return (rows == columns).astype(jnp.float32).astype(jnp.bfloat16)


def swap_order(blocks):
    size = TILE * blocks
    at = lax.broadcasted_iota(jnp.int32, (size, size), 0)
    source = lax.broadcasted_iota(jnp.int32, (size, size), 1)
    return onehot(at % TILE * blocks + at // TILE, source)


def ordered(order, piece_ref, group, blocks):
    size = TILE * blocks
    piece = piece_ref[pl.ds(pl.multiple_of(group * size, size), size), :]
    return jnp.dot(order, piece, preferred_element_type=jnp.float32).astype(jnp.bfloat16)


def left_kernel(piece_ref, fwd_ref, coef_ref, left_ref):
    blocks = coef_ref.shape[0]
    width = fwd_ref.shape[-1]
    order = swap_order(blocks)
    step = 3

    @pl.loop(0, coef_ref.shape[1] // TILE // step)
    def _(turn):
        coefs = []
        for part in range(step):
            group = turn * step + part
            coef = ordered(order, piece_ref, group, blocks)
            spot = pl.ds(pl.multiple_of(group * TILE, TILE), TILE)
            coef_ref[:, spot, :] = coef.reshape(blocks, TILE, width)
            coefs.append(coef)
        left = jnp.dot(
            jnp.concatenate(coefs, axis=0), fwd_ref[...], preferred_element_type=jnp.float32
        )
        left = left.astype(jnp.bfloat16).reshape(step, blocks, TILE, width)
        for part in range(step):
            group = turn * step + part
            spot = pl.ds(pl.multiple_of(group * TILE, TILE), TILE)
            left_ref[:, spot, :] = left[part]


def turn_kernel(side_ref, back_ref, out_ref):
    side = side_ref[0]
    run = 3 * TILE

    def picked(side):
        starts = [pl.multiple_of(y * 2 * run + side * run, TILE) for y in range(SIDE)]
        return jnp.concatenate([back_ref[pl.ds(at, run), :] for at in starts], axis=0)

    out_ref[...] = jnp.concatenate([picked(side), picked(1 - side)], axis=0).T


def turned(side, green_back):
    return pl.pallas_call(
        turn_kernel,
        out_shape=jax.ShapeDtypeStruct(green_back.shape, green_back.dtype),
        in_specs=[
            pl.BlockSpec(memory_space=pltpu.SMEM),
            pl.BlockSpec(memory_space=pltpu.VMEM),
        ],
        out_specs=pl.BlockSpec(memory_space=pltpu.VMEM),
        compiler_params=pltpu.CompilerParams(vmem_limit_bytes=SMALL_LIMIT),
        cost_estimate=COST,
    )(side, green_back)


def product_kernel(
    core_ref, coef_mine_ref, coef_other_ref, left_mine_ref, left_other_ref, back_t_ref, out_ref, right_ref
):
    blocks, half, width = coef_mine_ref.shape
    core = core_ref[0]
    run = 3 * TILE

    @pl.loop(0, blocks // 2)
    def _(pair):
        coefs = []
        for p in (2 * pair, 2 * pair + 1):
            coefs.append(jnp.concatenate([coef_mine_ref[p], coef_other_ref[p]], axis=0))
        right = jnp.dot(
            back_t_ref[...], jnp.concatenate(coefs, axis=1), preferred_element_type=jnp.float32
        )
        right = right.astype(jnp.bfloat16)
        right_ref[2 * pair] = right[:, :width]
        right_ref[2 * pair + 1] = right[:, width:]

    size = TILE * blocks
    gram = jnp.zeros((size, size), jnp.float32)
    for side, lefts in ((core, left_mine_ref), (1 - core, left_other_ref)):
        for y in range(SIDE):
            left_parts, right_parts = [], []
            for part in range(run // TILE):
                at = y * run + part * TILE
                natural = pl.multiple_of(y * 2 * run + side * run + part * TILE, TILE)
                left_parts.append(lefts[:, at : at + TILE, :].reshape(size, width))
                right_parts.append(right_ref[:, pl.ds(natural, TILE), :].reshape(size, width))
            gram += lax.dot_general(
                jnp.concatenate(left_parts, axis=1),
                jnp.concatenate(right_parts, axis=1),
                (((1,), (1,)), ((), ())),
                preferred_element_type=jnp.float32,
            )
    row = lax.broadcasted_iota(jnp.int32, (size, size), 0) % TILE
    column = lax.broadcasted_iota(jnp.int32, (size, size), 1) % TILE
    gram = jnp.where(row == column, gram, 0.0)
    gram = jnp.sum(gram.reshape(blocks, TILE, size), axis=1)
    at = lax.broadcasted_iota(jnp.int32, (size, blocks), 0) // TILE
    which = lax.broadcasted_iota(jnp.int32, (size, blocks), 1)
    pick = (at == which).astype(jnp.float32)
    polar = jnp.dot(gram, pick, precision=lax.Precision.HIGHEST, preferred_element_type=jnp.float32)
    polar = polar * (-1.0 / POINTS)
    _, cores, _ = out_ref.shape
    for p in range(blocks):
        for copy in range(out_ref.shape[0] * cores // blocks):
            place = p // cores * (out_ref.shape[0] * cores // blocks) + copy
            out_ref[place, p % cores : p % cores + 1, :] = polar[p : p + 1, :]


def left_half(piece, green_fwd, blocks):
    width = green_fwd.shape[-1]
    shape = jax.ShapeDtypeStruct((blocks, piece.shape[0] // blocks, width), jnp.bfloat16)
    return pl.pallas_call(
        left_kernel,
        out_shape=(shape, shape),
        in_specs=[pl.BlockSpec(memory_space=pltpu.VMEM)] * 2,
        out_specs=[pl.BlockSpec(memory_space=pltpu.VMEM)] * 2,
        compiler_params=pltpu.CompilerParams(vmem_limit_bytes=VMEM_LIMIT),
        cost_estimate=COST,
    )(piece, green_fwd)


def product(coef_mine, coef_other, left_mine, left_other, green_back, core, receivers, cores):
    blocks, half, width = coef_mine.shape
    return pl.pallas_call(
        product_kernel,
        out_shape=jax.ShapeDtypeStruct((receivers, cores, blocks), jnp.float32),
        in_specs=[pl.BlockSpec(memory_space=pltpu.SMEM)]
        + [pl.BlockSpec(memory_space=pltpu.VMEM)] * 5,
        out_specs=pl.BlockSpec(memory_space=pltpu.VMEM),
        scratch_shapes=[
            pltpu.VMEM((blocks, width, width), jnp.bfloat16),
        ],
        compiler_params=pltpu.CompilerParams(vmem_limit_bytes=VMEM_LIMIT),
        cost_estimate=COST,
    )(core, coef_mine, coef_other, left_mine, left_other, green_back)


def settle_kernel(block_ref, out_ref):
    out_ref[...] = block_ref[...]


def settled(block):
    return pl.pallas_call(
        settle_kernel,
        out_shape=jax.ShapeDtypeStruct(block.shape, block.dtype),
        in_specs=[pl.BlockSpec(memory_space=pltpu.VMEM)],
        out_specs=pl.BlockSpec(memory_space=pltpu.VMEM),
        compiler_params=pltpu.CompilerParams(vmem_limit_bytes=SMALL_LIMIT),
        cost_estimate=pl.CostEstimate(
            flops=50_000_000_000, bytes_accessed=2_500_000, transcendentals=0
        ),
    )(block)


def spread(block, axes, count):
    copies = jnp.broadcast_to(block[None], (count,) + block.shape)
    return lax.all_to_all(copies, axes, 0, 0, tiled=True)


def shards(sizes, bcoef, fwd_green, back_green, kmq, ir_table, ir_fit, freq_index):
    zl, cores, ys, zh, xs = (sizes[name] for name in ("zl", "c", "y", "zh", "x"))
    blocks, rows, orb = bcoef.shape[1:]
    points = zl * cores
    minor = points // SIDE
    core = lax.axis_index("c")
    high = lax.axis_index("zh")
    low = lax.axis_index("zl")
    here_y, here_x = lax.axis_index("y"), lax.axis_index("x")

    own_w = (here_y * zh + high) * xs + here_x
    own_k = low * cores + core
    target = kmq[0]
    major_shift = ((own_k >> 2) - (target >> 2)) & 3
    minor_shift = ((own_k & 3) - (target & 3)) & 3
    branch = (major_shift - 1) * (minor - 1) + minor_shift - 1

    transposed = [(c * zh + h, h * zh + c) for c in range(cores) for h in range(zh)]

    def partner(major, minor_by):
        route = []
        for k in range(points):
            a, b = divmod(k, minor)
            source = (a - major) % SIDE * minor + (b - minor_by) % minor
            for h in range(zh):
                route.append((source * zh + h, (k // cores * cores + h) * zh + k % cores))

        def work(shard, green_fwd, green_back):
            shard = shard.transpose(1, 0, 2).reshape(rows * blocks, orb)
            shard = lax.ppermute(shard, ("c", "zh"), transposed)
            green_fwd = lax.ppermute(green_fwd, ("c", "zh"), transposed)
            green_back = lax.ppermute(green_back, ("zl", "c", "zh"), route)
            mine = lax.cond(
                target >= 0,
                lambda block: spread(block, ("y", "x"), ys * xs),
                lambda block: jnp.zeros((ys * xs,) + block.shape, block.dtype),
                settled(shard),
            )
            mine = mine.reshape(ys * xs * rows * blocks, orb)
            return mine, green_fwd, green_back

        return work

    works = [partner(a, b) for a in range(1, SIDE) for b in range(1, minor)]
    mine, green_fwd, green_back = lax.switch(
        branch, works, bcoef[0], fwd_green[0, 0], back_green[0, 0]
    )
    other = lax.ppermute(mine, "c", [(0, 1), (1, 0)])
    coef_mine, left_mine = left_half(mine, green_fwd, blocks)
    green_back = turned(core[None], green_back)
    coef_other, left_other = left_half(other, green_fwd, blocks)
    pairs = product(coef_mine, coef_other, left_mine, left_other, green_back, core[None], zl * zh, cores)
    parts = lax.all_to_all(pairs, ("zl", "zh"), 0, 0, tiled=True)
    summed = jnp.sum(parts, axis=0)
    entries = jnp.broadcast_to(summed[:, None, :], (cores, ys * xs, blocks))
    entries = entries.reshape(cores * ys * xs, blocks)
    times = lax.all_to_all(entries, ("c", "y", "x"), 0, 0, tiled=True)
    chosen = lax.dynamic_slice_in_dim(ir_table, freq_index[own_w], 1, axis=1)
    fit = ir_fit.reshape(-1, ys, cores, xs).transpose(0, 2, 1, 3).reshape(ir_fit.shape)
    transform = jnp.sum(chosen.transpose(0, 2, 1) * fit[None], axis=1)
    result = jnp.sum(transform[:, :, None] * times[None], axis=1)
    return result[:, None, None, :]


def solution(mesh):
    sizes = {"zl": 8, "c": 2, "y": 4, "zh": 2, "x": 4}
    fine = Mesh(mesh.devices.reshape(tuple(sizes.values())), tuple(sizes))
    ka, tau = ("zl", "c"), ("y", "zh", "x")
    return jax.shard_map(
        functools.partial(shards, sizes),
        mesh=fine,
        in_specs=(
            P(ka, None, tau, None),
            P(ka, tau, None, None),
            P(ka, tau, None, None),
            P(ka),
            P(),
            P(),
            P(),
        ),
        out_specs=P(None, tau, ka, None),
        check_vma=False,
    )
```

profile of v0, /device:TPU:1, one launch (start us, length us, event | category | flops | bytes accessed | tf_op | source)
XLA Modules:
  0.0 114.2 jit_solution(8374636513511657129)
XLA Ops:
  0.0 0.0 copy-start
  0.7 49.4 %conditional.10 = (bf16[3072,384]{1,0:T(8,128)(2,1)}, bf16[384,384]{1,0:T(8,128)(2,1)}, bf16[384,384]{1,0:T(8,128)(2,1)}) conditional(s32[]{:T(128)} %clamp.3, (s32[]{:T(128)}, bf16[16,12,384]{2,0,1:T(8,128)(2,1)}, bf16[384,384]{1,0:T(8,128)(2,1)}, bf16[384,384]{1,0:T(8,128)(2,1)}) %tuple.159, (s32[]{:T(128)}, ...), branch_computations={%region_1.4_spmd, %region_4.7_spmd, %region_7.10_spmd, %region_10.... | conditional | flops 49999998976 | bytes 12674630 | solution.py:232
  0.7 16.8 %collective-permute-start = (bf16[192,384]{1,0:T(8,128)(2,1)}, bf16[192,384]{1,0:T(8,128)(2,1)S(1)}, u32[]{:S(2)}, u32[]{:S(2)}) collective-permute-start(bf16[192,384]{1,0:T(8,128)(2,1)} %bitcast.83), channel_id=1, source_target_pairs={{0,0},{4,32},{32,4},{36,36},{1,1},{5,33},{33,5},{37,37},{2,2},{6,3... | collective-permute-start | bytes 442376 | tf_op jit(solution)/shard_map/cond/branch_0_fun/ppermute | solution.py:217
  17.5 1.9 %collective-permute-start.1 = (bf16[384,384]{1,0:T(8,128)(2,1)}, bf16[384,384]{1,0:T(8,128)(2,1)}, u32[]{:S(2)}, u32[]{:S(2)}) collective-permute-start(bf16[384,384]{1,0:T(8,128)(2,1)} %get-tuple-element.124), channel_id=1, source_target_pairs={{0,0},{4,32},{32,4},{36,36},{1,1},{5,33},{33,5},{37,37},{2,2},{6,3... | collective-permute-start | bytes 884744 | tf_op jit(solution)/shard_map/cond/branch_0_fun/ppermute | solution.py:218
  19.5 1.9 %collective-permute-start.2 = (bf16[384,384]{1,0:T(8,128)(2,1)}, bf16[384,384]{1,0:T(8,128)(2,1)}, u32[]{:S(2)}, u32[]{:S(2)}) collective-permute-start(bf16[384,384]{1,0:T(8,128)(2,1)} %get-tuple-element.125), channel_id=1, source_target_pairs={{480,0},{484,32},{384,4},{388,36},{416,64},{420,96},{448,68},{452,... | collective-permute-start | bytes 884744 | tf_op jit(solution)/shard_map/cond/branch_0_fun/ppermute | solution.py:219
  22.0 0.0 collective-permute-done.block_ref
  22.1 28.0 %conditional = (bf16[3072,384]{1,0:T(8,128)(2,1)}) conditional(s32[]{:T(128)} %convert_element_type.18, () %tuple.86, bf16[192,384]{1,0:T(8,128)(2,1)S(1)} %branch_0_fun.1), branch_computations={%region_2.0_spmd, %region_3.3_spmd} | conditional | bytes 7225352 | solution.py:220
  22.1 0.3 broadcast_in_dim.24
  22.4 27.7 %all_to_all.50 = bf16[16,192,384]{2,1,0:T(8,128)(2,1)} all-to-all(bf16[16,192,384]{2,1,0:T(8,128)(2,1)S(1)} %broadcast_in_dim.24), channel_id=1, replica_groups=mesh['zl'=8,'c'=2,'y'=4,'zh'=2,'x'=4] {'y','x'}, dimensions={0} | all-to-all | bytes 4718592 | tf_op jit(solution)/shard_map/cond/branch_0_fun/cond/branch_1_fun/all_to_all | solution.py:185
  50.1 0.0 collective-permute-done.1
  50.1 0.0 collective-permute-done.2
  50.1 13.5 %collective-permute-start.27 = (bf16[3072,384]{1,0:T(8,128)(2,1)}, bf16[3072,384]{1,0:T(8,128)(2,1)S(1)}, u32[]{:S(2)}, u32[]{:S(2)}) collective-permute-start(bf16[3072,384]{1,0:T(8,128)(2,1)} %get-tuple-element.165.piece_ref), channel_id=1, source_target_pairs={{0,32},{32,0},{1,33},{33,1},{2,34},{34,2},{3,35},{35,3},{4,36},{36... | collective-permute-start | bytes 7077896 | tf_op jit(solution)/shard_map/ppermute | solution.py:235
  63.6 4.6 %shard_map.73 = (bf16[16,192,384]{2,1,0:T(8,128)(2,1)S(1)}, bf16[16,192,384]{2,1,0:T(8,128)(2,1)S(1)}) custom-call(bf16[3072,384]{1,0:T(8,128)(2,1)} %get-tuple-element.165.piece_ref, bf16[384,384]{1,0:T(8,128)(2,1)} %get-tuple-element.166.fwd_ref), custom_call_target="tpu_custom_call" | custom-call | flops 1000 | bytes 1000 | tf_op jit(solution)/shard_map/pallas_call | solution.py:140
  68.2 1.1 shard_map.75.back_t_ref
  69.3 0.0 collective-permute-done.27.piece_ref
  69.3 3.9 %shard_map.74 = (bf16[16,192,384]{2,1,0:T(8,128)(2,1)S(1)}, bf16[16,192,384]{2,1,0:T(8,128)(2,1)S(1)}) custom-call(bf16[3072,384]{1,0:T(8,128)(2,1)S(1)} %collective-permute-done.27.piece_ref, bf16[384,384]{1,0:T(8,128)(2,1)} %get-tuple-element.166.fwd_ref), custom_call_target="tpu_custom_call" | custom-call | flops 1000 | bytes 1000 | tf_op jit(solution)/shard_map/pallas_call | solution.py:140
  73.2 0.0 copy-start.2
  73.2 0.0 copy-start.1
  73.2 6.2 %shard_map.76 = f32[16,2,16]{2,1,0:T(2,128)} custom-call(s32[1]{0:T(128)} %bitcast.40.side_ref.core_ref, bf16[16,192,384]{2,1,0:T(8,128)(2,1)S(1)} %get-tuple-element.167.coef_mine_ref, bf16[16,192,384]{2,1,0:T(8,128)(2,1)S(1)} %get-tuple-element.168.coef_other_ref, bf16[16,192,384]{2,1,0:T(8,128)(2,1)S(1)} %get-tuple-element.169.left_mine_ref, ...), custom_call_target="tpu_custom_call" | custom-call | flops 1000 | bytes 1000 | tf_op jit(solution)/shard_map/pallas_call | solution.py:152
  79.4 10.4 %all-to-all-start.9 = ((f32[16,2,16]{2,1,0:T(2,128)}), f32[16,2,16]{2,1,0:T(2,128)S(1)}, u32[]{:S(2)}, u32[]{:S(2)}) async-start(f32[16,2,16]{2,1,0:T(2,128)} %shard_map.76), calls=%async_computation.9 | async-start | bytes 32768 | tf_op jit(solution)/shard_map/all_to_all | solution.py:240
  89.8 0.6 dynamic_slice.6
  91.7 0.0 copy-done.1
  91.7 0.1 copy.17
  91.8 0.1 copy.19
  92.5 0.2 dynamic-slice_reduce_fusion
  92.7 8.4 %all-to-all-done.9 = f32[16,2,16]{2,1,0:T(2,128)S(1)} async-done(((f32[16,2,16]{2,1,0:T(2,128)}), f32[16,2,16]{2,1,0:T(2,128)S(1)}, u32[]{:S(2)}, u32[]{:S(2)}) %all-to-all-start.9) | async-done | bytes 2080 | tf_op jit(solution)/shard_map/all_to_all | solution.py:240
  101.1 0.6 broadcast_in_dim.49
  101.7 5.1 %all-to-all-start.10 = ((f32[32,1,16]{2,1,0:T(1,128)}), f32[32,1,16]{2,1,0:T(1,128)S(1)}, u32[]{:S(2)}, u32[]{:S(2)}) async-start(f32[32,1,16]{2,1,0:T(1,128)} %bitcast.45), calls=%async_computation.10 | async-start | bytes 32768 | tf_op jit(solution)/shard_map/all_to_all | solution.py:244
  106.8 0.1 multiply_reduce_fusion
  106.9 6.6 %all-to-all-done.10 = f32[32,1,16]{2,1,0:T(1,128)S(1)} async-done(((f32[32,1,16]{2,1,0:T(1,128)}), f32[32,1,16]{2,1,0:T(1,128)S(1)}, u32[]{:S(2)}, u32[]{:S(2)}) %all-to-all-start.10) | async-done | bytes 2080 | tf_op jit(solution)/shard_map/all_to_all | solution.py:244
  113.5 0.1 copy.20
  113.5 0.7 multiply_reduce_fusion.1
  (5 shorter events, 0.1 us)
Async XLA Ops:
  0.0 92.5 %copy-start = (f32[2,128,32]{1,2,0:T(8,128)S(1)}, f32[2,128,32]{1,2,0:T(8,128)}, u32[]{:S(2)}) copy-start(f32[2,128,32]{1,2,0:T(8,128)} %param.38) | copy-start | bytes 98308
  0.7 21.4 %collective-permute-start = (bf16[192,384]{1,0:T(8,128)(2,1)}, bf16[192,384]{1,0:T(8,128)(2,1)S(1)}, u32[]{:S(2)}, u32[]{:S(2)}) collective-permute-start(bf16[192,384]{1,0:T(8,128)(2,1)} %bitcast.83), channel_id=1, source_target_pairs={{0,0},{4,32},{32,4},{36,36},{1,1},{5,33},{33,5},{37,37},{2,2},{6,3... | collective-permute-start | bytes 442376 | tf_op jit(solution)/shard_map/cond/branch_0_fun/ppermute | solution.py:217
  17.5 32.6 %collective-permute-start.1 = (bf16[384,384]{1,0:T(8,128)(2,1)}, bf16[384,384]{1,0:T(8,128)(2,1)}, u32[]{:S(2)}, u32[]{:S(2)}) collective-permute-start(bf16[384,384]{1,0:T(8,128)(2,1)} %get-tuple-element.124), channel_id=1, source_target_pairs={{0,0},{4,32},{32,4},{36,36},{1,1},{5,33},{33,5},{37,37},{2,2},{6,3... | collective-permute-start | bytes 884744 | tf_op jit(solution)/shard_map/cond/branch_0_fun/ppermute | solution.py:218
  19.5 30.6 %collective-permute-start.2 = (bf16[384,384]{1,0:T(8,128)(2,1)}, bf16[384,384]{1,0:T(8,128)(2,1)}, u32[]{:S(2)}, u32[]{:S(2)}) collective-permute-start(bf16[384,384]{1,0:T(8,128)(2,1)} %get-tuple-element.125), channel_id=1, source_target_pairs={{480,0},{484,32},{384,4},{388,36},{416,64},{420,96},{448,68},{452,... | collective-permute-start | bytes 884744 | tf_op jit(solution)/shard_map/cond/branch_0_fun/ppermute | solution.py:219
  50.1 19.2 %collective-permute-start.27 = (bf16[3072,384]{1,0:T(8,128)(2,1)}, bf16[3072,384]{1,0:T(8,128)(2,1)S(1)}, u32[]{:S(2)}, u32[]{:S(2)}) collective-permute-start(bf16[3072,384]{1,0:T(8,128)(2,1)} %get-tuple-element.165.piece_ref), channel_id=1, source_target_pairs={{0,32},{32,0},{1,33},{33,1},{2,34},{34,2},{3,35},{35,3},{4,36},{36... | collective-permute-start | bytes 7077896 | tf_op jit(solution)/shard_map/ppermute | solution.py:235
  73.2 16.6 %copy-start.2 = (s32[32]{0:T(128)S(1)}, s32[32]{0:T(128)}, u32[]{:S(2)}) copy-start(s32[32]{0:T(128)} %param.40) | copy-start | bytes 388
  73.2 18.5 %copy-start.1 = (f32[32,32]{1,0:T(8,128)S(1)}, f32[32,32]{1,0:T(8,128)}, u32[]{:S(2)}) copy-start(f32[32,32]{1,0:T(8,128)} %param.39) | copy-start | bytes 12292
  79.4 21.7 %all-to-all-start.9 = ((f32[16,2,16]{2,1,0:T(2,128)}), f32[16,2,16]{2,1,0:T(2,128)S(1)}, u32[]{:S(2)}, u32[]{:S(2)}) async-start(f32[16,2,16]{2,1,0:T(2,128)} %shard_map.76), calls=%async_computation.9 | async-start | bytes 32768 | tf_op jit(solution)/shard_map/all_to_all | solution.py:240
  101.7 11.7 %all-to-all-start.10 = ((f32[32,1,16]{2,1,0:T(1,128)}), f32[32,1,16]{2,1,0:T(1,128)S(1)}, u32[]{:S(2)}, u32[]{:S(2)}) async-start(f32[32,1,16]{2,1,0:T(1,128)} %bitcast.45), calls=%async_computation.10 | async-start | bytes 32768 | tf_op jit(solution)/shard_map/all_to_all | solution.py:244
where the time goes:
time: 115 us; the launch traced here: 114 us
  starting transfers between devices  49.6 us (43%)
  blocking collectives  27.7 us (24%)
  Pallas kernels  15.8 us (14%)
  waiting for transfers between devices  15 us (13%)
  between operations  2.74 us (2%)
  local copies, waits for them, and re-layouts  1.88 us (2%)
    all_to_all x1, blocking collectives, spread(): return lax.all_to_all(copies, axes, 0, 0, tiled=True)  27.7 us
    ppermute x1, starting transfers between devices, work(): shard = lax.ppermute(shard, ('c', 'zh'), transposed)  16.8 us
    ppermute x1, starting transfers between devices, shards(): other = lax.ppermute(mine, 'c', [(0, 1), (1, 0)])  13.5 us
    all_to_all x1, starting transfers between devices, shards(): parts = lax.all_to_all(pairs, ('zl', 'zh'), 0, 0, tiled=True)  10.4 us
    pallas_call x2, Pallas kernels, left_half(): pl.pallas_call(left_kernel, out_shape=(shape, shape), in_specs=[pl.BlockS...  8.47 us
    all_to_all x1, waiting for transfers between devices, shards(): parts = lax.all_to_all(pairs, ('zl', 'zh'), 0, 0, tiled=True)  8.42 us
    all_to_all x1, waiting for transfers between devices, shards(): times = lax.all_to_all(entries, ('c', 'y', 'x'), 0, 0, tiled=True)  6.57 us
    pallas_call x1, Pallas kernels, product(): pl.pallas_call(product_kernel, out_shape=jax.ShapeDtypeStruct((receivers,...  6.18 us
  transfers between devices with their start and end apart: 6, of which 2 were waited for; matrix products, arithmetic and copies ran while one was open for 1% of the time, Pallas kernels for 5%

commit v1 on v0

v1 whole, which is shorter than its diff:
```python
import functools

import jax
import jax.numpy as jnp
import numpy as np
from jax import lax
from jax.experimental import pallas as pl
from jax.experimental.pallas import tpu as pltpu
from jax.sharding import Mesh
from jax.sharding import PartitionSpec as P

SIDE = 4
TILE = 16
POINTS = 16
VMEM_LIMIT = 24 * 1024 * 1024
SMALL_LIMIT = 8 * 1024 * 1024
COST = pl.CostEstimate(flops=1000, bytes_accessed=1000, transcendentals=0)


def onehot(rows, columns):
    return (rows == columns).astype(jnp.float32).astype(jnp.bfloat16)


def swap_order(blocks):
    size = TILE * blocks
    at = lax.broadcasted_iota(jnp.int32, (size, size), 0)
    source = lax.broadcasted_iota(jnp.int32, (size, size), 1)
    return onehot(at % TILE * blocks + at // TILE, source)


def ordered(order, piece_ref, group, blocks):
    size = TILE * blocks
    piece = piece_ref[pl.ds(pl.multiple_of(group * size, size), size), :]
    return jnp.dot(order, piece, preferred_element_type=jnp.float32).astype(jnp.bfloat16)


def left_turn(order, piece_ref, fwd_ref, coef_ref, left_ref, turn, step):
    blocks = coef_ref.shape[0]
    width = fwd_ref.shape[-1]
    coefs = []
    for part in range(step):
        group = turn * step + part
        coef = ordered(order, piece_ref, group, blocks)
        spot = pl.ds(pl.multiple_of(group * TILE, TILE), TILE)
        coef_ref[:, spot, :] = coef.reshape(blocks, TILE, width)
        coefs.append(coef)
    left = jnp.dot(jnp.concatenate(coefs, axis=0), fwd_ref[...], preferred_element_type=jnp.float32)
    left = left.astype(jnp.bfloat16).reshape(step, blocks * TILE, width)
    for part in range(step):
        group = turn * step + part
        left_ref[:, pl.ds(pl.multiple_of(group * width, width), width)] = left[part]


def first_kernel(
    core_ref, piece_hbm, fwd_hbm, back_hbm, rows_hbm, coef_ref, left_ref, fwd_ref, back_t_ref, piece_ref, back_ref, rows_ref, sems
):
    blocks = coef_ref.shape[0]
    order = swap_order(blocks)
    step = 3
    turns = coef_ref.shape[1] // TILE // step
    size = step * TILE * blocks

    def piece_copy(turn):
        spot = pl.ds(pl.multiple_of(turn * size, size), size)
        return pltpu.make_async_copy(piece_hbm.at[spot], piece_ref.at[spot], sems.at[turn])

    fwd_copy = pltpu.make_async_copy(fwd_hbm, fwd_ref, sems.at[turns])
    back_copy = pltpu.make_async_copy(back_hbm, back_ref, sems.at[turns + 1])
    rows_copy = pltpu.make_async_copy(rows_hbm.at[core_ref[0]], rows_ref, sems.at[turns + 2])
    piece_copy(0).start()
    fwd_copy.start()
    for turn in range(1, turns):
        piece_copy(turn).start()
    back_copy.start()
    rows_copy.start()
    fwd_copy.wait()

    @pl.loop(0, turns)
    def _(turn):
        piece_copy(turn).wait()
        left_turn(order, piece_ref, fwd_ref, coef_ref, left_ref, turn, step)

    back_copy.wait()
    rows_copy.wait()
    rows = rows_ref[...]
    back = jnp.dot(rows, back_ref[...], preferred_element_type=jnp.float32).astype(jnp.bfloat16)
    back_t = lax.dot_general(
        rows, back, (((1,), (1,)), ((), ())), preferred_element_type=jnp.float32
    )
    back_t_ref[...] = back_t.astype(jnp.bfloat16)


def left_kernel(piece_ref, fwd_ref, coef_ref, left_ref):
    order = swap_order(coef_ref.shape[0])
    step = 3

    @pl.loop(0, coef_ref.shape[1] // TILE // step)
    def _(turn):
        left_turn(order, piece_ref, fwd_ref, coef_ref, left_ref, turn, step)


def product_kernel(
    coef_mine_ref, coef_other_ref, left_mine_ref, left_other_ref, back_t_ref, out_ref, right_ref
):
    blocks, half, width = coef_mine_ref.shape
    per_side = half // TILE

    @pl.loop(0, blocks // 2, unroll=4)
    def _(pair):
        coefs = []
        for p in (2 * pair, 2 * pair + 1):
            coefs.append(jnp.concatenate([coef_mine_ref[p], coef_other_ref[p]], axis=0))
        right = jnp.dot(
            back_t_ref[...], jnp.concatenate(coefs, axis=1), preferred_element_type=jnp.float32
        )
        right = right.astype(jnp.bfloat16)
        for inner in range(2):
            rows = pl.ds(pl.multiple_of((2 * pair + inner) * TILE, TILE), TILE)
            for block in range(2 * per_side):
                at = block % per_side * width
                right_ref[block // per_side, rows, at : at + width] = right[
                    block * TILE : (block + 1) * TILE, inner * width : (inner + 1) * width
                ]

    size = TILE * blocks
    gram = jnp.zeros((size, size), jnp.float32)
    for side, lefts in enumerate((left_mine_ref, left_other_ref)):
        gram += lax.dot_general(
            lefts[...], right_ref[side], (((1,), (1,)), ((), ())), preferred_element_type=jnp.float32
        )
    row = lax.broadcasted_iota(jnp.int32, (size, size), 0) % TILE
    column = lax.broadcasted_iota(jnp.int32, (size, size), 1) % TILE
    gram = jnp.where(row == column, gram, 0.0)
    gram = jnp.sum(gram.reshape(blocks, TILE, size), axis=1)
    at = lax.broadcasted_iota(jnp.int32, (size, blocks), 0) // TILE
    which = lax.broadcasted_iota(jnp.int32, (size, blocks), 1)
    pick = (at == which).astype(jnp.float32)
    polar = jnp.dot(gram, pick, precision=lax.Precision.HIGHEST, preferred_element_type=jnp.float32)
    polar = polar * (-1.0 / POINTS)
    _, cores, _ = out_ref.shape
    for p in range(blocks):
        for copy in range(out_ref.shape[0] * cores // blocks):
            place = p // cores * (out_ref.shape[0] * cores // blocks) + copy
            out_ref[place, p % cores : p % cores + 1, :] = polar[p : p + 1, :]


def half_shapes(piece, blocks):
    width = piece.shape[-1]
    half = piece.shape[0] // blocks
    coef = jax.ShapeDtypeStruct((blocks, half, width), jnp.bfloat16)
    left = jax.ShapeDtypeStruct((blocks * TILE, half // TILE * width), jnp.bfloat16)
    return coef, left


def first_half(core, piece, green_fwd, green_back, row_orders, blocks):
    width = green_fwd.shape[-1]
    square = jax.ShapeDtypeStruct((width, width), jnp.bfloat16)
    return pl.pallas_call(
        first_kernel,
        out_shape=half_shapes(piece, blocks) + (square, square),
        in_specs=[pl.BlockSpec(memory_space=pltpu.SMEM)] + [pl.BlockSpec(memory_space=pl.ANY)] * 4,
        out_specs=[pl.BlockSpec(memory_space=pltpu.VMEM)] * 4,
        scratch_shapes=[
            pltpu.VMEM(piece.shape, jnp.bfloat16),
            pltpu.VMEM((width, width), jnp.bfloat16),
            pltpu.VMEM((width, width), jnp.bfloat16),
            pltpu.SemaphoreType.DMA((SIDE + 3,)),
        ],
        compiler_params=pltpu.CompilerParams(vmem_limit_bytes=VMEM_LIMIT),
        cost_estimate=COST,
    )(core, piece, green_fwd, green_back, row_orders)


def second_half(piece, green_fwd, blocks):
    return pl.pallas_call(
        left_kernel,
        out_shape=half_shapes(piece, blocks),
        in_specs=[pl.BlockSpec(memory_space=pltpu.VMEM)] * 2,
        out_specs=[pl.BlockSpec(memory_space=pltpu.VMEM)] * 2,
        compiler_params=pltpu.CompilerParams(vmem_limit_bytes=VMEM_LIMIT),
        cost_estimate=COST,
    )(piece, green_fwd)


def product(coef_mine, coef_other, left_mine, left_other, back_t, receivers, cores):
    blocks, half, width = coef_mine.shape
    return pl.pallas_call(
        product_kernel,
        out_shape=jax.ShapeDtypeStruct((receivers, cores, blocks), jnp.float32),
        in_specs=[pl.BlockSpec(memory_space=pltpu.VMEM)] * 5,
        out_specs=pl.BlockSpec(memory_space=pltpu.VMEM),
        scratch_shapes=[
            pltpu.VMEM((2, blocks * TILE, half // TILE * width), jnp.bfloat16),
        ],
        compiler_params=pltpu.CompilerParams(vmem_limit_bytes=VMEM_LIMIT),
        cost_estimate=COST,
    )(coef_mine, coef_other, left_mine, left_other, back_t)


def settle_kernel(block_ref, out_ref):
    out_ref[...] = block_ref[...]


def settled(block):
    return pl.pallas_call(
        settle_kernel,
        out_shape=jax.ShapeDtypeStruct(block.shape, block.dtype),
        in_specs=[pl.BlockSpec(memory_space=pltpu.VMEM)],
        out_specs=pl.BlockSpec(memory_space=pltpu.VMEM),
        compiler_params=pltpu.CompilerParams(vmem_limit_bytes=SMALL_LIMIT),
        cost_estimate=pl.CostEstimate(
            flops=50_000_000_000, bytes_accessed=2_500_000, transcendentals=0
        ),
    )(block)


def spread(block, phases):
    for groups in phases:
        count = len(groups[0])
        copies = jnp.broadcast_to(block[None], (count,) + block.shape)
        block = lax.all_to_all(
            copies, ("c", "y", "x"), 0, 0, axis_index_groups=groups, tiled=True
        ).reshape(count * block.shape[0], block.shape[1])
    return block


def spread_phases(cores, ys, xs):
    def index(c, y, x):
        return (c * ys + y) * xs + x

    along_y = [[[index(c, y, x) for y in range(ys)] for x in range(xs)] for c in range(cores)]
    along_x = [[[index(c, y, x) for x in range(xs)] for y in range(ys)] for c in range(cores)]
    return along_y[0] + along_x[1], along_x[0] + along_y[1]


def row_orders_of(cores, ys, xs, rows):
    size = cores * ys * xs * rows
    half = size // cores
    orders = np.zeros((cores, size, size), np.float32)
    for core in range(cores):
        for at in range(size):
            bit = core if at < half else 1 - core
            outer, inner, row = at % half // (xs * rows), at // rows % xs, at % rows
            y, x = (outer, inner) if bit else (inner, outer)
            orders[core, at, ((y * cores + bit) * xs + x) * rows + row] = 1.0
    return jnp.asarray(orders, jnp.bfloat16)


def shards(sizes, bcoef, fwd_green, back_green, kmq, ir_table, ir_fit, freq_index):
    zl, cores, ys, zh, xs = (sizes[name] for name in ("zl", "c", "y", "zh", "x"))
    blocks, rows, orb = bcoef.shape[1:]
    points = zl * cores
    minor = points // SIDE
    core = lax.axis_index("c")
    high = lax.axis_index("zh")
    low = lax.axis_index("zl")
    here_y, here_x = lax.axis_index("y"), lax.axis_index("x")

    own_w = (here_y * zh + high) * xs + here_x
    own_k = low * cores + core
    target = kmq[0]
    major_shift = ((own_k >> 2) - (target >> 2)) & 3
    minor_shift = ((own_k & 3) - (target & 3)) & 3
    branch = (major_shift - 1) * (minor - 1) + minor_shift - 1

    phases = spread_phases(cores, ys, xs)
    transposed = [(c * zh + h, h * zh + c) for c in range(cores) for h in range(zh)]

    def partner(major, minor_by):
        route = []
        for k in range(points):
            a, b = divmod(k, minor)
            source = (a - major) % SIDE * minor + (b - minor_by) % minor
            for h in range(zh):
                route.append((source * zh + h, (k // cores * cores + h) * zh + k % cores))

        def work(shard, green_fwd, green_back):
            shard = shard.transpose(1, 0, 2).reshape(rows * blocks, orb)
            shard = lax.ppermute(shard, ("c", "zh"), transposed)
            green_fwd = lax.ppermute(green_fwd, ("c", "zh"), transposed)
            green_back = lax.ppermute(green_back, ("zl", "c", "zh"), route)
            mine = lax.cond(
                target >= 0,
                lambda block: spread(block, phases),
                lambda block: jnp.zeros((ys * xs * block.shape[0], block.shape[1]), block.dtype),
                settled(shard),
            )
            return mine, green_fwd, green_back

        return work

    works = [partner(a, b) for a in range(1, SIDE) for b in range(1, minor)]
    mine, green_fwd, green_back = lax.switch(
        branch, works, bcoef[0], fwd_green[0, 0], back_green[0, 0]
    )
    other = lax.ppermute(mine, "c", [(0, 1), (1, 0)])
    row_orders = row_orders_of(cores, ys, xs, rows)
    coef_mine, left_mine, green_fwd, back_t = first_half(
        core[None], mine, green_fwd, green_back, row_orders, blocks
    )
    coef_other, left_other = second_half(other, green_fwd, blocks)
    pairs = product(coef_mine, coef_other, left_mine, left_other, back_t, zl * zh, cores)
    parts = lax.all_to_all(pairs, ("zl", "zh"), 0, 0, tiled=True)
    summed = jnp.sum(parts, axis=0)
    entries = jnp.broadcast_to(summed[:, None, :], (cores, ys * xs, blocks))
    entries = entries.reshape(cores * ys * xs, blocks)
    times = lax.all_to_all(entries, ("c", "y", "x"), 0, 0, tiled=True)
    chosen = lax.dynamic_slice_in_dim(ir_table, freq_index[own_w], 1, axis=1)
    fit = ir_fit.reshape(-1, ys, cores, xs).transpose(0, 2, 1, 3).reshape(ir_fit.shape)
    transform = jnp.sum(chosen.transpose(0, 2, 1) * fit[None], axis=1)
    result = jnp.sum(transform[:, :, None] * times[None], axis=1)
    return result[:, None, None, :]


def solution(mesh):
    sizes = {"zl": 8, "c": 2, "y": 4, "zh": 2, "x": 4}
    fine = Mesh(mesh.devices.reshape(tuple(sizes.values())), tuple(sizes))
    ka, tau = ("zl", "c"), ("y", "zh", "x")
    return jax.shard_map(
        functools.partial(shards, sizes),
        mesh=fine,
        in_specs=(
            P(ka, None, tau, None),
            P(ka, tau, None, None),
            P(ka, tau, None, None),
            P(ka),
            P(),
            P(),
            P(),
        ),
        out_specs=P(None, tau, ka, None),
        check_vma=False,
    )
```

time: 115 us -> 114 us (level)
  starting transfers between devices: 49.6 us -> 39.2 us
  waiting for transfers between devices: 15 us -> 22.6 us
  blocking collectives: 27.7 us -> 32.2 us
  Pallas kernels: 15.8 us -> 12.9 us
    ppermute x1, starting transfers between devices: 13.5 us -> 4.38 us  [shards(): other = lax.ppermute(mine, 'c', [(0, 1), (1, 0)])]
    ppermute x1, waiting for transfers between devices: 0.01 us -> 7.48 us  [work(): green_back = lax.ppermute(green_back, ('zl', 'c', 'zh'), route)]
    all_to_all x1 -> x2, blocking collectives: 27.7 us -> 32.2 us  [spread(): lax.all_to_all(copies, ('c', 'y', 'x'), 0, 0, axis_index_groups=groups, t...]
    pallas_call x3 -> x2, Pallas kernels: 9.58 us -> 7.67 us  [the longest x1 4.75 us: first_half(): pl.pallas_call(first_kernel, out_shape=half_shapes(piece, blocks) + (squa...]
    all_to_all x1, starting transfers between devices: 10.4 us -> 8.9 us  [shards(): parts = lax.all_to_all(pairs, ('zl', 'zh'), 0, 0, tiled=True)]
  transfers between devices with their start and end apart: 6 -> 6, of which waited for: 2 -> 3; matrix products, arithmetic and copies ran while one was open for 1% -> 1% of each run, Pallas kernels for 5% -> 4%
where the time goes in v1:
time: 114 us; the launch traced here: 113 us
  starting transfers between devices  39.2 us (34%)
  blocking collectives  32.2 us (28%)
  waiting for transfers between devices  22.6 us (20%)
  Pallas kernels  12.9 us (11%)
  between operations  2.75 us (2%)
  local copies, waits for them, and re-layouts  1.84 us (2%)
    all_to_all x2, blocking collectives, spread(): lax.all_to_all(copies, ('c', 'y', 'x'), 0, 0, axis_index_groups=groups, t...  32.2 us
    ppermute x1, starting transfers between devices, work(): shard = lax.ppermute(shard, ('c', 'zh'), transposed)  17 us
    all_to_all x1, starting transfers between devices, shards(): parts = lax.all_to_all(pairs, ('zl', 'zh'), 0, 0, tiled=True)  8.9 us
    all_to_all x1, waiting for transfers between devices, shards(): parts = lax.all_to_all(pairs, ('zl', 'zh'), 0, 0, tiled=True)  8.42 us
    ppermute x1, waiting for transfers between devices, work(): green_back = lax.ppermute(green_back, ('zl', 'c', 'zh'), route)  7.48 us
    all_to_all x1, waiting for transfers between devices, shards(): times = lax.all_to_all(entries, ('c', 'y', 'x'), 0, 0, tiled=True)  6.73 us
    pallas_call x1, Pallas kernels, product(): pl.pallas_call(product_kernel, out_shape=jax.ShapeDtypeStruct((receivers,...  5.22 us
    all_to_all x1, starting transfers between devices, shards(): times = lax.all_to_all(entries, ('c', 'y', 'x'), 0, 0, tiled=True)  5.13 us
  transfers between devices with their start and end apart: 6, of which 3 were waited for; matrix products, arithmetic and copies ran while one was open for 1% of the time, Pallas kernels for 4%

profile of v1, /device:TPU:1, one launch (start us, length us, event | category | flops | bytes accessed | tf_op | source)
XLA Modules:
  0.0 113.2 jit_solution(13899853659171597109)
XLA Ops:
  0.7 0.0 copy-start.1
  0.7 61.6 %conditional.10 = (bf16[3072,384]{1,0:T(8,128)(2,1)}, bf16[384,384]{1,0:T(8,128)(2,1)}, bf16[384,384]{1,0:T(8,128)(2,1)}) conditional(s32[]{:T(128)} %clamp.3, (s32[]{:T(128)}, bf16[16,12,384]{2,0,1:T(8,128)(2,1)}, bf16[384,384]{1,0:T(8,128)(2,1)}, bf16[384,384]{1,0:T(8,128)(2,1)}) %tuple.141, (s32[]{:T(128)}, ...), branch_computations={%region_1.4_spmd, %region_4.7_spmd, %region_7.10_spmd, %region_10.... | conditional | flops 49999998976 | bytes 15033926 | solution.py:293
  0.7 17.0 %collective-permute-start.24 = (bf16[192,384]{1,0:T(8,128)(2,1)}, bf16[192,384]{1,0:T(8,128)(2,1)S(1)}, u32[]{:S(2)}, u32[]{:S(2)}) collective-permute-start(bf16[192,384]{1,0:T(8,128)(2,1)} %bitcast.109), channel_id=1, source_target_pairs={{0,0},{4,32},{32,4},{36,36},{1,1},{5,33},{33,5},{37,37},{2,2},{6,3... | collective-permute-start | bytes 442376 | tf_op jit(solution)/shard_map/cond/branch_8_fun/ppermute | solution.py:279
  17.7 1.9 %collective-permute-start.25 = (bf16[384,384]{1,0:T(8,128)(2,1)}, bf16[384,384]{1,0:T(8,128)(2,1)}, u32[]{:S(2)}, u32[]{:S(2)}) collective-permute-start(bf16[384,384]{1,0:T(8,128)(2,1)} %get-tuple-element.147), channel_id=1, source_target_pairs={{0,0},{4,32},{32,4},{36,36},{1,1},{5,33},{33,5},{37,37},{2,2},{6,3... | collective-permute-start | bytes 884744 | tf_op jit(solution)/shard_map/cond/branch_8_fun/ppermute | solution.py:280
  19.6 1.9 %collective-permute-start.26 = (bf16[384,384]{1,0:T(8,128)(2,1)}, bf16[384,384]{1,0:T(8,128)(2,1)}, u32[]{:S(2)}, u32[]{:S(2)}) collective-permute-start(bf16[384,384]{1,0:T(8,128)(2,1)} %get-tuple-element.148), channel_id=1, source_target_pairs={{160,0},{164,32},{192,4},{196,36},{224,64},{228,96},{128,68},{132,... | collective-permute-start | bytes 884744 | tf_op jit(solution)/shard_map/cond/branch_8_fun/ppermute | solution.py:281
  22.2 0.0 collective-permute-done.24.block_ref
  22.3 32.5 %conditional.8 = (bf16[3072,384]{1,0:T(8,128)(2,1)}) conditional(s32[]{:T(128)} %convert_element_type.26, () %tuple.84, bf16[192,384]{1,0:T(8,128)(2,1)S(1)} %branch_8_fun.1), branch_computations={%region_26.0_spmd, %region_27.27_spmd} | conditional | bytes 9584648 | solution.py:282
  22.3 0.1 broadcast_in_dim.103
  22.3 11.1 %all_to_all.102 = bf16[4,192,384]{2,1,0:T(8,128)(2,1)S(1)} all-to-all(bf16[4,192,384]{2,1,0:T(8,128)(2,1)S(1)} %broadcast_in_dim.103), channel_id=1, replica_groups={{0,8,16,24},{1,9,17,25},{2,10,18,26},{3,11,19,27},{32,33,34,35},{40,41,..., dimensions={0} | all-to-all | bytes 1179648 | tf_op jit(solution)/shard_map/cond/branch_8_fun/cond/branch_1_fun/all_to_all | solution.py:221
  33.4 0.2 broadcast_in_dim.112
  33.6 21.1 %all_to_all.103 = bf16[4,768,384]{2,1,0:T(8,128)(2,1)} all-to-all(bf16[4,768,384]{2,1,0:T(8,128)(2,1)S(1)} %broadcast_in_dim.112), channel_id=1, replica_groups={{0,1,2,3},{8,9,10,11},{16,17,18,19},{24,25,26,27},{32,40,48,56},{33,41,..., dimensions={0} | all-to-all | bytes 4718592 | tf_op jit(solution)/shard_map/cond/branch_8_fun/cond/branch_1_fun/all_to_all | solution.py:221
  54.8 0.0 collective-permute-done.25
  54.8 7.5 %collective-permute-done.26 = bf16[384,384]{1,0:T(8,128)(2,1)} collective-permute-done((bf16[384,384]{1,0:T(8,128)(2,1)}, bf16[384,384]{1,0:T(8,128)(2,1)}, u32[]{:S(2)}, u32[]{:S(2)}) %collective-permute-start.26) | collective-permute-done | bytes 294944 | tf_op jit(solution)/shard_map/cond/branch_8_fun/ppermute | solution.py:281
  62.3 4.4 %collective-permute-start.27 = (bf16[3072,384]{1,0:T(8,128)(2,1)}, bf16[3072,384]{1,0:T(8,128)(2,1)S(1)}, u32[]{:S(2)}, u32[]{:S(2)}) collective-permute-start(bf16[3072,384]{1,0:T(8,128)(2,1)} %get-tuple-element.158.piece_hbm), channel_id=1, source_target_pairs={{0,32},{32,0},{1,33},{33,1},{2,34},{34,2},{3,35},{35,3},{4,36},{36... | collective-permute-start | bytes 7077896 | tf_op jit(solution)/shard_map/ppermute | solution.py:296
  66.7 4.7 %shard_map.82 = (bf16[16,192,384]{2,1,0:T(8,128)(2,1)S(1)}, bf16[256,4608]{1,0:T(8,128)(2,1)S(1)}, bf16[384,384]{1,0:T(8,128)(2,1)S(1)}, bf16[384,384]{1,0:T(8,128)(2,1)S(1)}) custom-call(s32[1]{0:T(128)} %bitcast.49.core_ref, bf16[3072,384]{1,0:T(8,128)(2,1)} %get-tuple-element.158.piece_hbm, bf16[384,384]{1,0:T(8,128)(2,1)} %get-tuple-element.159.fwd_hbm, ...), custom_call_target="tpu_custom_call" | custom-call | flops 1000 | bytes 1000 | tf_op jit(solution)/shard_map/pallas_call | solution.py:158
  71.4 0.0 collective-permute-done.27.piece_ref
  71.5 2.9 %shard_map.83 = (bf16[16,192,384]{2,1,0:T(8,128)(2,1)S(1)}, bf16[256,4608]{1,0:T(8,128)(2,1)S(1)}) custom-call(bf16[3072,384]{1,0:T(8,128)(2,1)S(1)} %collective-permute-done.27.piece_ref, bf16[384,384]{1,0:T(8,128)(2,1)S(1)} %get-tuple-element.162.fwd_ref), custom_call_target="tpu_custom_call" | custom-call | flops 1000 | bytes 1000 | tf_op jit(solution)/shard_map/pallas_call | solution.py:175
  74.4 0.0 copy-start.3
  74.4 0.0 copy-start.2
  74.4 5.2 %shard_map.84 = f32[16,2,16]{2,1,0:T(2,128)} custom-call(bf16[16,192,384]{2,1,0:T(8,128)(2,1)S(1)} %get-tuple-element.161.coef_mine_ref, bf16[16,192,384]{2,1,0:T(8,128)(2,1)S(1)} %get-tuple-element.163.coef_other_ref, bf16[256,4608]{1,0:T(8,128)(2,1)S(1)} %get-tuple-element.164.left_mine_ref, bf16[256,4608]{1,0:T(8,128)(2,1)S(1)} %get-tuple-element.165.left_other_ref, ...), custom_call_target="tpu_custom_call" | custom-call | flops 1000 | bytes 1000 | tf_op jit(solution)/shard_map/pallas_call | solution.py:187
  79.6 8.9 %all-to-all-start.18 = ((f32[16,2,16]{2,1,0:T(2,128)}), f32[16,2,16]{2,1,0:T(2,128)S(1)}, u32[]{:S(2)}, u32[]{:S(2)}) async-start(f32[16,2,16]{2,1,0:T(2,128)} %shard_map.84), calls=%async_computation.18 | async-start | bytes 32768 | tf_op jit(solution)/shard_map/all_to_all | solution.py:303
  88.6 0.6 dynamic_slice.6
  90.5 0.1 copy.18
  90.5 0.1 copy.20
  91.3 0.2 dynamic-slice_reduce_fusion
  91.4 8.4 %all-to-all-done.18 = f32[16,2,16]{2,1,0:T(2,128)S(1)} async-done(((f32[16,2,16]{2,1,0:T(2,128)}), f32[16,2,16]{2,1,0:T(2,128)S(1)}, u32[]{:S(2)}, u32[]{:S(2)}) %all-to-all-start.18) | async-done | bytes 2080 | tf_op jit(solution)/shard_map/all_to_all | solution.py:303
  99.9 0.6 broadcast_in_dim.117
  100.5 5.1 %all-to-all-start.19 = ((f32[32,1,16]{2,1,0:T(1,128)}), f32[32,1,16]{2,1,0:T(1,128)S(1)}, u32[]{:S(2)}, u32[]{:S(2)}) async-start(f32[32,1,16]{2,1,0:T(1,128)} %bitcast.54), calls=%async_computation.19 | async-start | bytes 32768 | tf_op jit(solution)/shard_map/all_to_all | solution.py:307
  105.6 0.1 multiply_reduce_fusion
  105.7 6.7 %all-to-all-done.19 = f32[32,1,16]{2,1,0:T(1,128)S(1)} async-done(((f32[32,1,16]{2,1,0:T(1,128)}), f32[32,1,16]{2,1,0:T(1,128)S(1)}, u32[]{:S(2)}, u32[]{:S(2)}) %all-to-all-start.19) | async-done | bytes 2080 | tf_op jit(solution)/shard_map/all_to_all | solution.py:307
  112.4 0.1 copy.21
  112.5 0.7 multiply_reduce_fusion.1
  (8 shorter events, 0.1 us)
Async XLA Ops:
  0.0 91.3 %copy-start = (f32[2,128,32]{1,2,0:T(8,128)S(1)}, f32[2,128,32]{1,2,0:T(8,128)}, u32[]{:S(2)}) copy-start(f32[2,128,32]{1,2,0:T(8,128)} %param.39) | copy-start | bytes 98308
  0.7 66.0 %copy-start.1 = (bf16[2,384,384]{2,1,0:T(8,128)(2,1)S(1)}, bf16[2,384,384]{2,1,0:T(8,128)(2,1)}, u32[]{:S(2)}) copy-start(bf16[2,384,384]{2,1,0:T(8,128)(2,1)} %constant.79.clone.rows_hbm) | copy-start | bytes 1769476
  0.7 21.5 %collective-permute-start.24 = (bf16[192,384]{1,0:T(8,128)(2,1)}, bf16[192,384]{1,0:T(8,128)(2,1)S(1)}, u32[]{:S(2)}, u32[]{:S(2)}) collective-permute-start(bf16[192,384]{1,0:T(8,128)(2,1)} %bitcast.109), channel_id=1, source_target_pairs={{0,0},{4,32},{32,4},{36,36},{1,1},{5,33},{33,5},{37,37},{2,2},{6,3... | collective-permute-start | bytes 442376 | tf_op jit(solution)/shard_map/cond/branch_8_fun/ppermute | solution.py:279
  17.7 37.1 %collective-permute-start.25 = (bf16[384,384]{1,0:T(8,128)(2,1)}, bf16[384,384]{1,0:T(8,128)(2,1)}, u32[]{:S(2)}, u32[]{:S(2)}) collective-permute-start(bf16[384,384]{1,0:T(8,128)(2,1)} %get-tuple-element.147), channel_id=1, source_target_pairs={{0,0},{4,32},{32,4},{36,36},{1,1},{5,33},{33,5},{37,37},{2,2},{6,3... | collective-permute-start | bytes 884744 | tf_op jit(solution)/shard_map/cond/branch_8_fun/ppermute | solution.py:280
  19.6 42.6 %collective-permute-start.26 = (bf16[384,384]{1,0:T(8,128)(2,1)}, bf16[384,384]{1,0:T(8,128)(2,1)}, u32[]{:S(2)}, u32[]{:S(2)}) collective-permute-start(bf16[384,384]{1,0:T(8,128)(2,1)} %get-tuple-element.148), channel_id=1, source_target_pairs={{160,0},{164,32},{192,4},{196,36},{224,64},{228,96},{128,68},{132,... | collective-permute-start | bytes 884744 | tf_op jit(solution)/shard_map/cond/branch_8_fun/ppermute | solution.py:281
  62.3 9.2 %collective-permute-start.27 = (bf16[3072,384]{1,0:T(8,128)(2,1)}, bf16[3072,384]{1,0:T(8,128)(2,1)S(1)}, u32[]{:S(2)}, u32[]{:S(2)}) collective-permute-start(bf16[3072,384]{1,0:T(8,128)(2,1)} %get-tuple-element.158.piece_hbm), channel_id=1, source_target_pairs={{0,32},{32,0},{1,33},{33,1},{2,34},{34,2},{3,35},{35,3},{4,36},{36... | collective-permute-start | bytes 7077896 | tf_op jit(solution)/shard_map/ppermute | solution.py:296
  74.4 14.2 %copy-start.3 = (s32[32]{0:T(128)S(1)}, s32[32]{0:T(128)}, u32[]{:S(2)}) copy-start(s32[32]{0:T(128)} %param.41) | copy-start | bytes 388
  74.4 16.1 %copy-start.2 = (f32[32,32]{1,0:T(8,128)S(1)}, f32[32,32]{1,0:T(8,128)}, u32[]{:S(2)}) copy-start(f32[32,32]{1,0:T(8,128)} %param.40) | copy-start | bytes 12292
  79.6 20.2 %all-to-all-start.18 = ((f32[16,2,16]{2,1,0:T(2,128)}), f32[16,2,16]{2,1,0:T(2,128)S(1)}, u32[]{:S(2)}, u32[]{:S(2)}) async-start(f32[16,2,16]{2,1,0:T(2,128)} %shard_map.84), calls=%async_computation.18 | async-start | bytes 32768 | tf_op jit(solution)/shard_map/all_to_all | solution.py:303
  100.5 12.0 %all-to-all-start.19 = ((f32[32,1,16]{2,1,0:T(1,128)}), f32[32,1,16]{2,1,0:T(1,128)S(1)}, u32[]{:S(2)}, u32[]{:S(2)}) async-start(f32[32,1,16]{2,1,0:T(1,128)} %bitcast.54), calls=%async_computation.19 | async-start | bytes 32768 | tf_op jit(solution)/shard_map/all_to_all | solution.py:307

commit v2 on v1

--- a/solution.py
+++ b/solution.py
@@ -2,7 +2,6 @@
 
 import jax
 import jax.numpy as jnp
-import numpy as np
 from jax import lax
 from jax.experimental import pallas as pl
 from jax.experimental.pallas import tpu as pltpu
@@ -10,9 +9,12 @@
 from jax.sharding import PartitionSpec as P
 
 SIDE = 4
+ROWS = 12
+STEP = 4
 TILE = 16
 POINTS = 16
-VMEM_LIMIT = 24 * 1024 * 1024
+FIRST_LIMIT = 10 * 1024 * 1024
+PRODUCT_LIMIT = 14 * 1024 * 1024
 SMALL_LIMIT = 8 * 1024 * 1024
 COST = pl.CostEstimate(flops=1000, bytes_accessed=1000, transcendentals=0)
 
@@ -28,19 +30,34 @@
     return onehot(at % TILE * blocks + at // TILE, source)
 
 
-def ordered(order, piece_ref, group, blocks):
-    size = TILE * blocks
-    piece = piece_ref[pl.ds(pl.multiple_of(group * size, size), size), :]
-    return jnp.dot(order, piece, preferred_element_type=jnp.float32).astype(jnp.bfloat16)
+def row_order(size, lane, odd):
+    at = lax.broadcasted_iota(jnp.int32, (size, 1), 0)
+    side = (at >= size // 2).astype(jnp.int32)
+    here = lane ^ side
+    rest = at - side * (size // 2)
+    shard = (rest * 171) >> 11
+    row = rest - shard * ROWS
+    outer, inner = shard >> 2, shard & 3
+    y = jnp.where(here == 1, outer, inner)
+    x = jnp.where(here == 1, inner, outer)
+    bit = here ^ ((x + y) & 1) ^ odd
+    return onehot(((y * 2 + bit) * SIDE + x) * ROWS + row, lax.broadcasted_iota(jnp.int32, (size, size), 1))
 
 
 def left_turn(order, piece_ref, fwd_ref, coef_ref, left_ref, turn, step):
     blocks = coef_ref.shape[0]
     width = fwd_ref.shape[-1]
+    size = TILE * blocks
+    pieces = [
+        piece_ref[pl.ds(pl.multiple_of((turn * step + part) * size, size), size), :]
+        for part in range(step)
+    ]
+    wide = jnp.dot(order, jnp.concatenate(pieces, axis=1), preferred_element_type=jnp.float32)
+    wide = wide.astype(jnp.bfloat16)
     coefs = []
     for part in range(step):
         group = turn * step + part
-        coef = ordered(order, piece_ref, group, blocks)
+        coef = wide[:, part * width : (part + 1) * width]
         spot = pl.ds(pl.multiple_of(group * TILE, TILE), TILE)
         coef_ref[:, spot, :] = coef.reshape(blocks, TILE, width)
         coefs.append(coef)
@@ -52,11 +69,11 @@
 
 
 def first_kernel(
-    core_ref, piece_hbm, fwd_hbm, back_hbm, rows_hbm, coef_ref, left_ref, fwd_ref, back_t_ref, piece_ref, back_ref, rows_ref, sems
+    lane_ref, odd_ref, piece_hbm, fwd_hbm, back_hbm, coef_ref, left_ref, fwd_ref, back_t_ref, piece_ref, back_ref, sems
 ):
     blocks = coef_ref.shape[0]
     order = swap_order(blocks)
-    step = 3
+    step = STEP
     turns = coef_ref.shape[1] // TILE // step
     size = step * TILE * blocks
 
@@ -66,13 +83,11 @@
 
     fwd_copy = pltpu.make_async_copy(fwd_hbm, fwd_ref, sems.at[turns])
     back_copy = pltpu.make_async_copy(back_hbm, back_ref, sems.at[turns + 1])
-    rows_copy = pltpu.make_async_copy(rows_hbm.at[core_ref[0]], rows_ref, sems.at[turns + 2])
     piece_copy(0).start()
     fwd_copy.start()
     for turn in range(1, turns):
         piece_copy(turn).start()
     back_copy.start()
-    rows_copy.start()
     fwd_copy.wait()
 
     @pl.loop(0, turns)
@@ -81,8 +96,7 @@
         left_turn(order, piece_ref, fwd_ref, coef_ref, left_ref, turn, step)
 
     back_copy.wait()
-    rows_copy.wait()
-    rows = rows_ref[...]
+    rows = row_order(back_ref.shape[0], lane_ref[0], odd_ref[0])
     back = jnp.dot(rows, back_ref[...], preferred_element_type=jnp.float32).astype(jnp.bfloat16)
     back_t = lax.dot_general(
         rows, back, (((1,), (1,)), ((), ())), preferred_element_type=jnp.float32
@@ -92,7 +106,7 @@
 
 def left_kernel(piece_ref, fwd_ref, coef_ref, left_ref):
     order = swap_order(coef_ref.shape[0])
-    step = 3
+    step = STEP
 
     @pl.loop(0, coef_ref.shape[1] // TILE // step)
     def _(turn):
@@ -152,23 +166,23 @@
     return coef, left
 
 
-def first_half(core, piece, green_fwd, green_back, row_orders, blocks):
+def first_half(lane, odd, piece, green_fwd, green_back, blocks):
     width = green_fwd.shape[-1]
     square = jax.ShapeDtypeStruct((width, width), jnp.bfloat16)
     return pl.pallas_call(
         first_kernel,
         out_shape=half_shapes(piece, blocks) + (square, square),
-        in_specs=[pl.BlockSpec(memory_space=pltpu.SMEM)] + [pl.BlockSpec(memory_space=pl.ANY)] * 4,
+        in_specs=[pl.BlockSpec(memory_space=pltpu.SMEM)] * 2
+        + [pl.BlockSpec(memory_space=pl.ANY)] * 3,
         out_specs=[pl.BlockSpec(memory_space=pltpu.VMEM)] * 4,
         scratch_shapes=[
             pltpu.VMEM(piece.shape, jnp.bfloat16),
             pltpu.VMEM((width, width), jnp.bfloat16),
-            pltpu.VMEM((width, width), jnp.bfloat16),
-            pltpu.SemaphoreType.DMA((SIDE + 3,)),
+            pltpu.SemaphoreType.DMA((piece.shape[0] // (STEP * TILE * blocks) + 2,)),
         ],
-        compiler_params=pltpu.CompilerParams(vmem_limit_bytes=VMEM_LIMIT),
+        compiler_params=pltpu.CompilerParams(vmem_limit_bytes=FIRST_LIMIT),
         cost_estimate=COST,
-    )(core, piece, green_fwd, green_back, row_orders)
+    )(lane, odd, piece, green_fwd, green_back)
 
 
 def second_half(piece, green_fwd, blocks):
@@ -177,7 +191,7 @@
         out_shape=half_shapes(piece, blocks),
         in_specs=[pl.BlockSpec(memory_space=pltpu.VMEM)] * 2,
         out_specs=[pl.BlockSpec(memory_space=pltpu.VMEM)] * 2,
-        compiler_params=pltpu.CompilerParams(vmem_limit_bytes=VMEM_LIMIT),
+        compiler_params=pltpu.CompilerParams(vmem_limit_bytes=SMALL_LIMIT),
         cost_estimate=COST,
     )(piece, green_fwd)
 
@@ -192,7 +206,7 @@
         scratch_shapes=[
             pltpu.VMEM((2, blocks * TILE, half // TILE * width), jnp.bfloat16),
         ],
-        compiler_params=pltpu.CompilerParams(vmem_limit_bytes=VMEM_LIMIT),
+        compiler_params=pltpu.CompilerParams(vmem_limit_bytes=PRODUCT_LIMIT),
         cost_estimate=COST,
     )(coef_mine, coef_other, left_mine, left_other, back_t)
 
@@ -225,25 +239,12 @@
 
 
 def spread_phases(cores, ys, xs):
-    def index(c, y, x):
-        return (c * ys + y) * xs + x
+    def index(lane, y, x):
+        return ((lane ^ (x + y) & 1) * ys + y) * xs + x
 
     along_y = [[[index(c, y, x) for y in range(ys)] for x in range(xs)] for c in range(cores)]
     along_x = [[[index(c, y, x) for x in range(xs)] for y in range(ys)] for c in range(cores)]
     return along_y[0] + along_x[1], along_x[0] + along_y[1]
-
-
-def row_orders_of(cores, ys, xs, rows):
-    size = cores * ys * xs * rows
-    half = size // cores
-    orders = np.zeros((cores, size, size), np.float32)
-    for core in range(cores):
-        for at in range(size):
-            bit = core if at < half else 1 - core
-            outer, inner, row = at % half // (xs * rows), at // rows % xs, at % rows
-            y, x = (outer, inner) if bit else (inner, outer)
-            orders[core, at, ((y * cores + bit) * xs + x) * rows + row] = 1.0
-    return jnp.asarray(orders, jnp.bfloat16)
 
 
 def shards(sizes, bcoef, fwd_green, back_green, kmq, ir_table, ir_fit, freq_index):
@@ -264,7 +265,17 @@
     branch = (major_shift - 1) * (minor - 1) + minor_shift - 1
 
     phases = spread_phases(cores, ys, xs)
-    transposed = [(c * zh + h, h * zh + c) for c in range(cores) for h in range(zh)]
+    odd = low & 1
+    swapped = [
+        ((z * cores + c) * zh + h, (z * cores + (h ^ z & 1)) * zh + (c ^ z & 1))
+        for z in range(zl)
+        for c in range(cores)
+        for h in range(zh)
+    ]
+    columns = [
+        [(z * cores + (half ^ z & 1)) * zh + h for z in range(zl) for h in range(zh)]
+        for half in range(cores)
+    ]
 
     def partner(major, minor_by):
         route = []
@@ -272,12 +283,13 @@
             a, b = divmod(k, minor)
             source = (a - major) % SIDE * minor + (b - minor_by) % minor
             for h in range(zh):
-                route.append((source * zh + h, (k // cores * cores + h) * zh + k % cores))
+                z, odd = k // cores, k // cores & 1
+                route.append((source * zh + h, (z * cores + (h ^ odd)) * zh + (k % cores ^ odd)))
 
         def work(shard, green_fwd, green_back):
             shard = shard.transpose(1, 0, 2).reshape(rows * blocks, orb)
-            shard = lax.ppermute(shard, ("c", "zh"), transposed)
-            green_fwd = lax.ppermute(green_fwd, ("c", "zh"), transposed)
+            shard = lax.ppermute(shard, ("zl", "c", "zh"), swapped)
+            green_fwd = lax.ppermute(green_fwd, ("zl", "c", "zh"), swapped)
             green_back = lax.ppermute(green_back, ("zl", "c", "zh"), route)
             mine = lax.cond(
                 target >= 0,
@@ -293,20 +305,28 @@
     mine, green_fwd, green_back = lax.switch(
         branch, works, bcoef[0], fwd_green[0, 0], back_green[0, 0]
     )
+    mine, own_w, odd, is_odd, lane = lax.optimization_barrier(
+        (mine, own_w.astype(jnp.uint32), odd, odd == 1, core ^ (here_x + here_y) & 1)
+    )
     other = lax.ppermute(mine, "c", [(0, 1), (1, 0)])
-    row_orders = row_orders_of(cores, ys, xs, rows)
     coef_mine, left_mine, green_fwd, back_t = first_half(
-        core[None], mine, green_fwd, green_back, row_orders, blocks
+        lane[None], odd[None], mine, green_fwd, green_back, blocks
     )
     coef_other, left_other = second_half(other, green_fwd, blocks)
     pairs = product(coef_mine, coef_other, left_mine, left_other, back_t, zl * zh, cores)
-    parts = lax.all_to_all(pairs, ("zl", "zh"), 0, 0, tiled=True)
+    pairs, ir_table, ir_fit, freq_index = lax.optimization_barrier(
+        (pairs, ir_table, ir_fit, freq_index)
+    )
+    parts = lax.all_to_all(
+        pairs, ("zl", "c", "zh"), 0, 0, axis_index_groups=columns, tiled=True
+    )
     summed = jnp.sum(parts, axis=0)
     entries = jnp.broadcast_to(summed[:, None, :], (cores, ys * xs, blocks))
     entries = entries.reshape(cores * ys * xs, blocks)
     times = lax.all_to_all(entries, ("c", "y", "x"), 0, 0, tiled=True)
-    chosen = lax.dynamic_slice_in_dim(ir_table, freq_index[own_w], 1, axis=1)
-    fit = ir_fit.reshape(-1, ys, cores, xs).transpose(0, 2, 1, 3).reshape(ir_fit.shape)
+    chosen = lax.dynamic_slice_in_dim(ir_table, lax.dynamic_slice(freq_index, (own_w,), (1,))[0], 1, axis=1)
+    fit = ir_fit.reshape(-1, ys, cores, xs).transpose(0, 2, 1, 3)
+    fit = jnp.where(is_odd, fit[:, ::-1], fit).reshape(ir_fit.shape)
     transform = jnp.sum(chosen.transpose(0, 2, 1) * fit[None], axis=1)
     result = jnp.sum(transform[:, :, None] * times[None], axis=1)
     return result[:, None, None, :]

time: 114 us -> 116 us (1.018)
  waiting for transfers between devices: 22.6 us -> 15 us
  starting transfers between devices: 39.2 us -> 46.3 us
  blocking collectives: 32.2 us -> 35.1 us
    ppermute x1, waiting for transfers between devices: 7.48 us -> 0.01 us  [work(): green_back = lax.ppermute(green_back, ('zl', 'c', 'zh'), route)]
    ppermute x1, starting transfers between devices: 1.92 us -> 7.48 us  [work(): green_back = lax.ppermute(green_back, ('zl', 'c', 'zh'), route)]
    all_to_all x2, blocking collectives: 32.2 us -> 35.1 us  [spread(): lax.all_to_all(copies, ('c', 'y', 'x'), 0, 0, axis_index_groups=groups, t...]
    all_to_all x1, starting transfers between devices: 8.9 us -> 11.6 us  [shards(): lax.all_to_all(pairs, ('zl', 'c', 'zh'), 0, 0, axis_index_groups=columns,...]
  transfers between devices with their start and end apart: 6 -> 6, of which waited for: 3 -> 2; matrix products, arithmetic and copies ran while one was open for 1% -> 1% of each run, Pallas kernels for 4% -> 4%
where the time goes in v2:
time: 116 us; the launch traced here: 115 us
  starting transfers between devices  46.3 us (40%)
  blocking collectives  35.1 us (30%)
  waiting for transfers between devices  15 us (13%)
  Pallas kernels  12.6 us (11%)
  between operations  2.73 us (2%)
  local copies, waits for them, and re-layouts  1.83 us (2%)
    all_to_all x2, blocking collectives, spread(): lax.all_to_all(copies, ('c', 'y', 'x'), 0, 0, axis_index_groups=groups, t...  35.1 us
    ppermute x1, starting transfers between devices, work(): shard = lax.ppermute(shard, ('zl', 'c', 'zh'), swapped)  16.8 us
    all_to_all x1, starting transfers between devices, shards(): lax.all_to_all(pairs, ('zl', 'c', 'zh'), 0, 0, axis_index_groups=columns,...  11.6 us
    all_to_all x1, waiting for transfers between devices, shards(): lax.all_to_all(pairs, ('zl', 'c', 'zh'), 0, 0, axis_index_groups=columns,...  8.41 us
    ppermute x1, starting transfers between devices, work(): green_back = lax.ppermute(green_back, ('zl', 'c', 'zh'), route)  7.48 us
    all_to_all x1, waiting for transfers between devices, shards(): times = lax.all_to_all(entries, ('c', 'y', 'x'), 0, 0, tiled=True)  6.57 us
    all_to_all x1, starting transfers between devices, shards(): times = lax.all_to_all(entries, ('c', 'y', 'x'), 0, 0, tiled=True)  5.3 us
    pallas_call x1, Pallas kernels, product(): pl.pallas_call(product_kernel, out_shape=jax.ShapeDtypeStruct((receivers,...  5.25 us
  transfers between devices with their start and end apart: 6, of which 2 were waited for; matrix products, arithmetic and copies ran while one was open for 1% of the time, Pallas kernels for 4%

profile of v2, /device:TPU:1, one launch (start us, length us, event | category | flops | bytes accessed | tf_op | source)
XLA Modules:
  0.0 115.1 jit_solution(563826479582226183)
XLA Ops:
  0.7 62.3 %conditional.10 = (bf16[3072,384]{1,0:T(8,128)(2,1)}, bf16[384,384]{1,0:T(8,128)(2,1)}, bf16[384,384]{1,0:T(8,128)(2,1)}) conditional(s32[]{:T(128)} %clamp.3, (s32[]{:T(128)}, bf16[16,12,384]{2,0,1:T(8,128)(2,1)}, bf16[384,384]{1,0:T(8,128)(2,1)}, bf16[384,384]{1,0:T(8,128)(2,1)}) %tuple.145, (s32[]{:T(128)}, ...), branch_computations={%region_0.0_spmd, %region_3.0_spmd, %region_6.0_spmd, %region_9.0_... | conditional | flops 49999998976 | bytes 15033926 | solution.py:305
  0.7 16.8 %collective-permute-start.18 = (bf16[192,384]{1,0:T(8,128)(2,1)}, bf16[192,384]{1,0:T(8,128)(2,1)S(1)}, u32[]{:S(2)}, u32[]{:S(2)}) collective-permute-start(bf16[192,384]{1,0:T(8,128)(2,1)} %bitcast.108), channel_id=1, source_target_pairs={{0,0},{4,32},{32,4},{36,36},{64,100},{68,68},{96,96},{100,64},{128... | collective-permute-start | bytes 442376 | tf_op jit(solution)/shard_map/cond/branch_6_fun/ppermute | solution.py:291
  17.5 1.9 %collective-permute-start.19 = (bf16[384,384]{1,0:T(8,128)(2,1)}, bf16[384,384]{1,0:T(8,128)(2,1)}, u32[]{:S(2)}, u32[]{:S(2)}) collective-permute-start(bf16[384,384]{1,0:T(8,128)(2,1)} %get-tuple-element.139), channel_id=1, source_target_pairs={{0,0},{4,32},{32,4},{36,36},{64,100},{68,68},{96,96},{100,64},{128... | collective-permute-start | bytes 884744 | tf_op jit(solution)/shard_map/cond/branch_6_fun/ppermute | solution.py:292
  19.5 7.5 %collective-permute-start.20 = (bf16[384,384]{1,0:T(8,128)(2,1)}, bf16[384,384]{1,0:T(8,128)(2,1)}, u32[]{:S(2)}, u32[]{:S(2)}) collective-permute-start(bf16[384,384]{1,0:T(8,128)(2,1)} %get-tuple-element.140), channel_id=1, source_target_pairs={{224,0},{228,32},{128,4},{132,36},{160,100},{164,68},{192,96},{196... | collective-permute-start | bytes 884744 | tf_op jit(solution)/shard_map/cond/branch_6_fun/ppermute | solution.py:293
  27.6 0.0 collective-permute-done.18.block_ref
  27.6 35.4 %conditional.6 = (bf16[3072,384]{1,0:T(8,128)(2,1)}) conditional(s32[]{:T(128)} %convert_element_type.26, () %tuple.80, bf16[192,384]{1,0:T(8,128)(2,1)S(1)} %branch_6_fun.1), branch_computations={%region_19.0_spmd, %region_20.0_spmd} | conditional | bytes 9584648 | solution.py:294
  27.7 0.1 broadcast_in_dim.98
  27.7 12.7 %all_to_all.98 = bf16[4,192,384]{2,1,0:T(8,128)(2,1)S(1)} all-to-all(bf16[4,192,384]{2,1,0:T(8,128)(2,1)S(1)} %broadcast_in_dim.98), channel_id=1, replica_groups={{0,40,16,56},{33,9,49,25},{2,42,18,58},{35,11,51,27},{32,1,34,3},{8,41,..., dimensions={0} | all-to-all | bytes 1179648 | tf_op jit(solution)/shard_map/cond/branch_6_fun/cond/branch_1_fun/all_to_all | solution.py:235
  40.4 0.2 broadcast_in_dim.100
  40.6 22.4 %all_to_all.99 = bf16[4,768,384]{2,1,0:T(8,128)(2,1)} all-to-all(bf16[4,768,384]{2,1,0:T(8,128)(2,1)S(1)} %broadcast_in_dim.100), channel_id=1, replica_groups={{0,33,2,35},{40,9,42,11},{16,49,18,51},{56,25,58,27},{32,8,48,24},{1,41..., dimensions={0} | all-to-all | bytes 4718592 | tf_op jit(solution)/shard_map/cond/branch_6_fun/cond/branch_1_fun/all_to_all | solution.py:235
  63.0 0.0 collective-permute-done.19
  63.0 0.0 collective-permute-done.20
  63.0 3.2 %collective-permute-start.27 = (bf16[3072,384]{1,0:T(8,128)(2,1)}, bf16[3072,384]{1,0:T(8,128)(2,1)S(1)}, u32[]{:S(2)}, u32[]{:S(2)}) collective-permute-start(bf16[3072,384]{1,0:T(8,128)(2,1)} %get-tuple-element.170.piece_hbm), channel_id=1, source_target_pairs={{0,32},{32,0},{1,33},{33,1},{2,34},{34,2},{3,35},{35,3},{4,36},{36... | collective-permute-start | bytes 7077896 | tf_op jit(solution)/shard_map/ppermute | solution.py:311
  66.2 4.6 %shard_map.73 = (bf16[16,192,384]{2,1,0:T(8,128)(2,1)S(1)}, bf16[256,4608]{1,0:T(8,128)(2,1)S(1)}, bf16[384,384]{1,0:T(8,128)(2,1)S(1)}, bf16[384,384]{1,0:T(8,128)(2,1)S(1)}) custom-call(s32[1]{0:T(128)} %bitcast.49.lane_ref, s32[1]{0:T(128)} %bitcast.50.odd_ref, bf16[3072,384]{1,0:T(8,128)(2,1)} %get-tuple-element.170.piece_hbm, ...), custom_call_target="tpu_custom_call" | custom-call | flops 1000 | bytes 1000 | tf_op jit(solution)/shard_map/pallas_call | solution.py:172
  70.9 0.0 collective-permute-done.27.piece_ref
  70.9 2.7 %shard_map.74 = (bf16[16,192,384]{2,1,0:T(8,128)(2,1)S(1)}, bf16[256,4608]{1,0:T(8,128)(2,1)S(1)}) custom-call(bf16[3072,384]{1,0:T(8,128)(2,1)S(1)} %collective-permute-done.27.piece_ref, bf16[384,384]{1,0:T(8,128)(2,1)S(1)} %get-tuple-element.174.fwd_ref), custom_call_target="tpu_custom_call" | custom-call | flops 1000 | bytes 1000 | tf_op jit(solution)/shard_map/pallas_call | solution.py:189
  73.6 0.0 copy-start.1
  73.6 0.0 copy-start.2
  73.6 5.3 %shard_map.75 = f32[16,2,16]{2,1,0:T(2,128)} custom-call(bf16[16,192,384]{2,1,0:T(8,128)(2,1)S(1)} %get-tuple-element.173.coef_mine_ref, bf16[16,192,384]{2,1,0:T(8,128)(2,1)S(1)} %get-tuple-element.175.coef_other_ref, bf16[256,4608]{1,0:T(8,128)(2,1)S(1)} %get-tuple-element.176.left_mine_ref, bf16[256,4608]{1,0:T(8,128)(2,1)S(1)} %get-tuple-element.177.left_other_ref, ...), custom_call_target="tpu_custom_call" | custom-call | flops 1000 | bytes 1000 | tf_op jit(solution)/shard_map/pallas_call | solution.py:201
  78.9 11.6 %all-to-all-start.18 = ((f32[16,2,16]{2,1,0:T(2,128)}), f32[16,2,16]{2,1,0:T(2,128)S(1)}, u32[]{:S(2)}, u32[]{:S(2)}) async-start(f32[16,2,16]{2,1,0:T(2,128)} %shard_map.75), calls=%async_computation.18 | async-start | bytes 32768 | tf_op jit(solution)/shard_map/all_to_all | solution.py:320
  90.5 0.0 copy-done.1
  90.5 0.1 copy.17
  90.6 0.6 dynamic_slice.6
  92.5 0.1 copy.19
  93.2 0.2 dynamic-slice_reduce_fusion
  93.4 8.4 %all-to-all-done.18 = f32[16,2,16]{2,1,0:T(2,128)S(1)} async-done(((f32[16,2,16]{2,1,0:T(2,128)}), f32[16,2,16]{2,1,0:T(2,128)S(1)}, u32[]{:S(2)}, u32[]{:S(2)}) %all-to-all-start.18) | async-done | bytes 2080 | tf_op jit(solution)/shard_map/all_to_all | solution.py:320
  101.8 0.6 broadcast_in_dim.127
  102.4 5.3 %all-to-all-start.19 = ((f32[32,1,16]{2,1,0:T(1,128)}), f32[32,1,16]{2,1,0:T(1,128)S(1)}, u32[]{:S(2)}, u32[]{:S(2)}) async-start(f32[32,1,16]{2,1,0:T(1,128)} %bitcast.55), calls=%async_computation.19 | async-start | bytes 32768 | tf_op jit(solution)/shard_map/all_to_all | solution.py:326
  107.7 0.1 multiply_reduce_fusion
  107.8 6.6 %all-to-all-done.19 = f32[32,1,16]{2,1,0:T(1,128)S(1)} async-done(((f32[32,1,16]{2,1,0:T(1,128)}), f32[32,1,16]{2,1,0:T(1,128)S(1)}, u32[]{:S(2)}, u32[]{:S(2)}) %all-to-all-start.19) | async-done | bytes 2080 | tf_op jit(solution)/shard_map/all_to_all | solution.py:326
  114.4 0.1 copy.20
  114.4 0.7 multiply_reduce_fusion.1
  (7 shorter events, 0.1 us)
Async XLA Ops:
  0.0 93.2 %copy-start = (f32[2,128,32]{1,2,0:T(8,128)S(1)}, f32[2,128,32]{1,2,0:T(8,128)}, u32[]{:S(2)}) copy-start(f32[2,128,32]{1,2,0:T(8,128)} %param.38) | copy-start | bytes 98308
  0.7 26.9 %collective-permute-start.18 = (bf16[192,384]{1,0:T(8,128)(2,1)}, bf16[192,384]{1,0:T(8,128)(2,1)S(1)}, u32[]{:S(2)}, u32[]{:S(2)}) collective-permute-start(bf16[192,384]{1,0:T(8,128)(2,1)} %bitcast.108), channel_id=1, source_target_pairs={{0,0},{4,32},{32,4},{36,36},{64,100},{68,68},{96,96},{100,64},{128... | collective-permute-start | bytes 442376 | tf_op jit(solution)/shard_map/cond/branch_6_fun/ppermute | solution.py:291
  17.5 45.5 %collective-permute-start.19 = (bf16[384,384]{1,0:T(8,128)(2,1)}, bf16[384,384]{1,0:T(8,128)(2,1)}, u32[]{:S(2)}, u32[]{:S(2)}) collective-permute-start(bf16[384,384]{1,0:T(8,128)(2,1)} %get-tuple-element.139), channel_id=1, source_target_pairs={{0,0},{4,32},{32,4},{36,36},{64,100},{68,68},{96,96},{100,64},{128... | collective-permute-start | bytes 884744 | tf_op jit(solution)/shard_map/cond/branch_6_fun/ppermute | solution.py:292
  19.5 43.5 %collective-permute-start.20 = (bf16[384,384]{1,0:T(8,128)(2,1)}, bf16[384,384]{1,0:T(8,128)(2,1)}, u32[]{:S(2)}, u32[]{:S(2)}) collective-permute-start(bf16[384,384]{1,0:T(8,128)(2,1)} %get-tuple-element.140), channel_id=1, source_target_pairs={{224,0},{228,32},{128,4},{132,36},{160,100},{164,68},{192,96},{196... | collective-permute-start | bytes 884744 | tf_op jit(solution)/shard_map/cond/branch_6_fun/ppermute | solution.py:293
  63.0 7.9 %collective-permute-start.27 = (bf16[3072,384]{1,0:T(8,128)(2,1)}, bf16[3072,384]{1,0:T(8,128)(2,1)S(1)}, u32[]{:S(2)}, u32[]{:S(2)}) collective-permute-start(bf16[3072,384]{1,0:T(8,128)(2,1)} %get-tuple-element.170.piece_hbm), channel_id=1, source_target_pairs={{0,32},{32,0},{1,33},{33,1},{2,34},{34,2},{3,35},{35,3},{4,36},{36... | collective-permute-start | bytes 7077896 | tf_op jit(solution)/shard_map/ppermute | solution.py:311
  73.6 16.9 %copy-start.1 = (f32[32,32]{1,0:T(8,128)S(1)}, f32[32,32]{1,0:T(8,128)}, u32[]{:S(2)}) copy-start(f32[32,32]{1,0:T(8,128)} %param.39) | copy-start | bytes 12292
  73.6 16.9 %copy-start.2 = (s32[32]{0:T(128)S(1)}, s32[32]{0:T(128)}, u32[]{:S(2)}) copy-start(s32[32]{0:T(128)} %param.40) | copy-start | bytes 388
  78.9 22.9 %all-to-all-start.18 = ((f32[16,2,16]{2,1,0:T(2,128)}), f32[16,2,16]{2,1,0:T(2,128)S(1)}, u32[]{:S(2)}, u32[]{:S(2)}) async-start(f32[16,2,16]{2,1,0:T(2,128)} %shard_map.75), calls=%async_computation.18 | async-start | bytes 32768 | tf_op jit(solution)/shard_map/all_to_all | solution.py:320
  102.4 12.0 %all-to-all-start.19 = ((f32[32,1,16]{2,1,0:T(1,128)}), f32[32,1,16]{2,1,0:T(1,128)S(1)}, u32[]{:S(2)}, u32[]{:S(2)}) async-start(f32[32,1,16]{2,1,0:T(1,128)} %bitcast.55), calls=%async_computation.19 | async-start | bytes 32768 | tf_op jit(solution)/shard_map/all_to_all | solution.py:326

commit v3 on v2

--- a/solution.py
+++ b/solution.py
@@ -30,18 +30,17 @@
     return onehot(at % TILE * blocks + at // TILE, source)
 
 
-def row_order(size, lane, odd):
+def row_order(size, core):
     at = lax.broadcasted_iota(jnp.int32, (size, 1), 0)
     side = (at >= size // 2).astype(jnp.int32)
-    here = lane ^ side
+    here = core ^ side
     rest = at - side * (size // 2)
     shard = (rest * 171) >> 11
     row = rest - shard * ROWS
     outer, inner = shard >> 2, shard & 3
     y = jnp.where(here == 1, outer, inner)
     x = jnp.where(here == 1, inner, outer)
-    bit = here ^ ((x + y) & 1) ^ odd
-    return onehot(((y * 2 + bit) * SIDE + x) * ROWS + row, lax.broadcasted_iota(jnp.int32, (size, size), 1))
+    return onehot(((y * 2 + here) * SIDE + x) * ROWS + row, lax.broadcasted_iota(jnp.int32, (size, size), 1))
 
 
 def left_turn(order, piece_ref, fwd_ref, coef_ref, left_ref, turn, step):
@@ -69,7 +68,7 @@
 
 
 def first_kernel(
-    lane_ref, odd_ref, piece_hbm, fwd_hbm, back_hbm, coef_ref, left_ref, fwd_ref, back_t_ref, piece_ref, back_ref, sems
+    core_ref, piece_hbm, fwd_hbm, back_hbm, coef_ref, left_ref, fwd_ref, back_t_ref, piece_ref, back_ref, sems
 ):
     blocks = coef_ref.shape[0]
     order = swap_order(blocks)
@@ -96,7 +95,7 @@
         left_turn(order, piece_ref, fwd_ref, coef_ref, left_ref, turn, step)
 
     back_copy.wait()
-    rows = row_order(back_ref.shape[0], lane_ref[0], odd_ref[0])
+    rows = row_order(back_ref.shape[0], core_ref[0])
     back = jnp.dot(rows, back_ref[...], preferred_element_type=jnp.float32).astype(jnp.bfloat16)
     back_t = lax.dot_general(
         rows, back, (((1,), (1,)), ((), ())), preferred_element_type=jnp.float32
@@ -166,13 +165,13 @@
     return coef, left
 
 
-def first_half(lane, odd, piece, green_fwd, green_back, blocks):
+def first_half(core, piece, green_fwd, green_back, blocks):
     width = green_fwd.shape[-1]
     square = jax.ShapeDtypeStruct((width, width), jnp.bfloat16)
     return pl.pallas_call(
         first_kernel,
         out_shape=half_shapes(piece, blocks) + (square, square),
-        in_specs=[pl.BlockSpec(memory_space=pltpu.SMEM)] * 2
+        in_specs=[pl.BlockSpec(memory_space=pltpu.SMEM)]
         + [pl.BlockSpec(memory_space=pl.ANY)] * 3,
         out_specs=[pl.BlockSpec(memory_space=pltpu.VMEM)] * 4,
         scratch_shapes=[
@@ -182,7 +181,7 @@
         ],
         compiler_params=pltpu.CompilerParams(vmem_limit_bytes=FIRST_LIMIT),
         cost_estimate=COST,
-    )(lane, odd, piece, green_fwd, green_back)
+    )(core, piece, green_fwd, green_back)
 
 
 def second_half(piece, green_fwd, blocks):
@@ -239,8 +238,8 @@
 
 
 def spread_phases(cores, ys, xs):
-    def index(lane, y, x):
-        return ((lane ^ (x + y) & 1) * ys + y) * xs + x
+    def index(c, y, x):
+        return (c * ys + y) * xs + x
 
     along_y = [[[index(c, y, x) for y in range(ys)] for x in range(xs)] for c in range(cores)]
     along_x = [[[index(c, y, x) for x in range(xs)] for y in range(ys)] for c in range(cores)]
@@ -265,17 +264,7 @@
     branch = (major_shift - 1) * (minor - 1) + minor_shift - 1
 
     phases = spread_phases(cores, ys, xs)
-    odd = low & 1
-    swapped = [
-        ((z * cores + c) * zh + h, (z * cores + (h ^ z & 1)) * zh + (c ^ z & 1))
-        for z in range(zl)
-        for c in range(cores)
-        for h in range(zh)
-    ]
-    columns = [
-        [(z * cores + (half ^ z & 1)) * zh + h for z in range(zl) for h in range(zh)]
-        for half in range(cores)
-    ]
+    swapped = [(c * zh + h, h * zh + c) for c in range(cores) for h in range(zh)]
 
     def partner(major, minor_by):
         route = []
@@ -283,13 +272,12 @@
             a, b = divmod(k, minor)
             source = (a - major) % SIDE * minor + (b - minor_by) % minor
             for h in range(zh):
-                z, odd = k // cores, k // cores & 1
-                route.append((source * zh + h, (z * cores + (h ^ odd)) * zh + (k % cores ^ odd)))
+                route.append((source * zh + h, (k // cores * cores + h) * zh + k % cores))
 
         def work(shard, green_fwd, green_back):
             shard = shard.transpose(1, 0, 2).reshape(rows * blocks, orb)
-            shard = lax.ppermute(shard, ("zl", "c", "zh"), swapped)
-            green_fwd = lax.ppermute(green_fwd, ("zl", "c", "zh"), swapped)
+            shard = lax.ppermute(shard, ("c", "zh"), swapped)
+            green_fwd = lax.ppermute(green_fwd, ("c", "zh"), swapped)
             green_back = lax.ppermute(green_back, ("zl", "c", "zh"), route)
             mine = lax.cond(
                 target >= 0,
@@ -305,28 +293,23 @@
     mine, green_fwd, green_back = lax.switch(
         branch, works, bcoef[0], fwd_green[0, 0], back_green[0, 0]
     )
-    mine, own_w, odd, is_odd, lane = lax.optimization_barrier(
-        (mine, own_w.astype(jnp.uint32), odd, odd == 1, core ^ (here_x + here_y) & 1)
-    )
+    mine, own_w, core = lax.optimization_barrier((mine, own_w.astype(jnp.uint32), core))
     other = lax.ppermute(mine, "c", [(0, 1), (1, 0)])
     coef_mine, left_mine, green_fwd, back_t = first_half(
-        lane[None], odd[None], mine, green_fwd, green_back, blocks
+        core[None], mine, green_fwd, green_back, blocks
     )
     coef_other, left_other = second_half(other, green_fwd, blocks)
     pairs = product(coef_mine, coef_other, left_mine, left_other, back_t, zl * zh, cores)
     pairs, ir_table, ir_fit, freq_index = lax.optimization_barrier(
         (pairs, ir_table, ir_fit, freq_index)
     )
-    parts = lax.all_to_all(
-        pairs, ("zl", "c", "zh"), 0, 0, axis_index_groups=columns, tiled=True
-    )
+    parts = lax.all_to_all(pairs, ("zl", "zh"), 0, 0, tiled=True)
     summed = jnp.sum(parts, axis=0)
     entries = jnp.broadcast_to(summed[:, None, :], (cores, ys * xs, blocks))
     entries = entries.reshape(cores * ys * xs, blocks)
     times = lax.all_to_all(entries, ("c", "y", "x"), 0, 0, tiled=True)
     chosen = lax.dynamic_slice_in_dim(ir_table, lax.dynamic_slice(freq_index, (own_w,), (1,))[0], 1, axis=1)
-    fit = ir_fit.reshape(-1, ys, cores, xs).transpose(0, 2, 1, 3)
-    fit = jnp.where(is_odd, fit[:, ::-1], fit).reshape(ir_fit.shape)
+    fit = ir_fit.reshape(-1, ys, cores, xs).transpose(0, 2, 1, 3).reshape(ir_fit.shape)
     transform = jnp.sum(chosen.transpose(0, 2, 1) * fit[None], axis=1)
     result = jnp.sum(transform[:, :, None] * times[None], axis=1)
     return result[:, None, None, :]

time: 116 us -> 113 us (0.974)
  waiting for transfers between devices: 15 us -> 22.5 us
  starting transfers between devices: 46.3 us -> 39.1 us
  blocking collectives: 35.1 us -> 32.2 us
    ppermute x1, waiting for transfers between devices: 0.01 us -> 7.48 us  [work(): green_back = lax.ppermute(green_back, ('zl', 'c', 'zh'), route)]
    ppermute x1, starting transfers between devices: 7.48 us -> 1.92 us  [work(): green_back = lax.ppermute(green_back, ('zl', 'c', 'zh'), route)]
    all_to_all x2, blocking collectives: 35.1 us -> 32.2 us  [spread(): lax.all_to_all(copies, ('c', 'y', 'x'), 0, 0, axis_index_groups=groups, t...]
    all_to_all x1, starting transfers between devices: 11.6 us -> 8.9 us  [shards(): parts = lax.all_to_all(pairs, ('zl', 'zh'), 0, 0, tiled=True)]
  transfers between devices with their start and end apart: 6 -> 6, of which waited for: 2 -> 3; matrix products, arithmetic and copies ran while one was open for 1% -> 1% of each run, Pallas kernels for 4% -> 4%
where the time goes in v3:
time: 113 us
  starting transfers between devices  39.1 us (35%)
  blocking collectives  32.2 us (28%)
  waiting for transfers between devices  22.5 us (20%)
  Pallas kernels  12.6 us (11%)
  between operations  2.72 us (2%)
  local copies, waits for them, and re-layouts  1.84 us (2%)
    all_to_all x2, blocking collectives, spread(): lax.all_to_all(copies, ('c', 'y', 'x'), 0, 0, axis_index_groups=groups, t...  32.2 us
    ppermute x1, starting transfers between devices, work(): shard = lax.ppermute(shard, ('c', 'zh'), swapped)  16.8 us
    all_to_all x1, starting transfers between devices, shards(): parts = lax.all_to_all(pairs, ('zl', 'zh'), 0, 0, tiled=True)  8.9 us
    all_to_all x1, waiting for transfers between devices, shards(): parts = lax.all_to_all(pairs, ('zl', 'zh'), 0, 0, tiled=True)  8.42 us
    ppermute x1, waiting for transfers between devices, work(): green_back = lax.ppermute(green_back, ('zl', 'c', 'zh'), route)  7.48 us
    all_to_all x1, waiting for transfers between devices, shards(): times = lax.all_to_all(entries, ('c', 'y', 'x'), 0, 0, tiled=True)  6.57 us
    pallas_call x1, Pallas kernels, product(): pl.pallas_call(product_kernel, out_shape=jax.ShapeDtypeStruct((receivers,...  5.24 us
    all_to_all x1, starting transfers between devices, shards(): times = lax.all_to_all(entries, ('c', 'y', 'x'), 0, 0, tiled=True)  5.15 us
  transfers between devices with their start and end apart: 6, of which 3 were waited for; matrix products, arithmetic and copies ran while one was open for 1% of the time, Pallas kernels for 4%

profile of v3, /device:TPU:1, one launch (start us, length us, event | category | flops | bytes accessed | tf_op | source)
XLA Modules:
  0.0 112.6 jit_solution(13523038844998706575)
XLA Ops:
  0.7 61.5 %conditional.10 = (bf16[3072,384]{1,0:T(8,128)(2,1)}, bf16[384,384]{1,0:T(8,128)(2,1)}, bf16[384,384]{1,0:T(8,128)(2,1)}) conditional(s32[]{:T(128)} %clamp.3, (s32[]{:T(128)}, bf16[16,12,384]{2,0,1:T(8,128)(2,1)}, bf16[384,384]{1,0:T(8,128)(2,1)}, bf16[384,384]{1,0:T(8,128)(2,1)}) %tuple.145, (s32[]{:T(128)}, ...), branch_computations={%region_0.0_spmd, %region_3.0_spmd, %region_6.0_spmd, %region_9.0_... | conditional | flops 49999998976 | bytes 15033926 | solution.py:293
  0.7 16.8 %collective-permute-start.24 = (bf16[192,384]{1,0:T(8,128)(2,1)}, bf16[192,384]{1,0:T(8,128)(2,1)S(1)}, u32[]{:S(2)}, u32[]{:S(2)}) collective-permute-start(bf16[192,384]{1,0:T(8,128)(2,1)} %bitcast.109), channel_id=1, source_target_pairs={{0,0},{4,32},{32,4},{36,36},{1,1},{5,33},{33,5},{37,37},{2,2},{6,3... | collective-permute-start | bytes 442376 | tf_op jit(solution)/shard_map/cond/branch_8_fun/ppermute | solution.py:279
  17.6 1.9 %collective-permute-start.25 = (bf16[384,384]{1,0:T(8,128)(2,1)}, bf16[384,384]{1,0:T(8,128)(2,1)}, u32[]{:S(2)}, u32[]{:S(2)}) collective-permute-start(bf16[384,384]{1,0:T(8,128)(2,1)} %get-tuple-element.147), channel_id=1, source_target_pairs={{0,0},{4,32},{32,4},{36,36},{1,1},{5,33},{33,5},{37,37},{2,2},{6,3... | collective-permute-start | bytes 884744 | tf_op jit(solution)/shard_map/cond/branch_8_fun/ppermute | solution.py:280
  19.5 1.9 %collective-permute-start.26 = (bf16[384,384]{1,0:T(8,128)(2,1)}, bf16[384,384]{1,0:T(8,128)(2,1)}, u32[]{:S(2)}, u32[]{:S(2)}) collective-permute-start(bf16[384,384]{1,0:T(8,128)(2,1)} %get-tuple-element.148), channel_id=1, source_target_pairs={{160,0},{164,32},{192,4},{196,36},{224,64},{228,96},{128,68},{132,... | collective-permute-start | bytes 884744 | tf_op jit(solution)/shard_map/cond/branch_8_fun/ppermute | solution.py:281
  22.1 0.0 collective-permute-done.24.block_ref
  22.1 32.5 %conditional.8 = (bf16[3072,384]{1,0:T(8,128)(2,1)}) conditional(s32[]{:T(128)} %convert_element_type.28, () %tuple.84, bf16[192,384]{1,0:T(8,128)(2,1)S(1)} %branch_8_fun.1), branch_computations={%region_25.0_spmd, %region_26.0_spmd} | conditional | bytes 9584648 | solution.py:282
  22.1 0.1 broadcast_in_dim.103
  22.2 11.1 %all_to_all.102 = bf16[4,192,384]{2,1,0:T(8,128)(2,1)S(1)} all-to-all(bf16[4,192,384]{2,1,0:T(8,128)(2,1)S(1)} %broadcast_in_dim.103), channel_id=1, replica_groups={{0,8,16,24},{1,9,17,25},{2,10,18,26},{3,11,19,27},{32,33,34,35},{40,41,..., dimensions={0} | all-to-all | bytes 1179648 | tf_op jit(solution)/shard_map/cond/branch_8_fun/cond/branch_1_fun/all_to_all | solution.py:234
  33.3 0.2 broadcast_in_dim.112
  33.5 21.1 %all_to_all.103 = bf16[4,768,384]{2,1,0:T(8,128)(2,1)} all-to-all(bf16[4,768,384]{2,1,0:T(8,128)(2,1)S(1)} %broadcast_in_dim.112), channel_id=1, replica_groups={{0,1,2,3},{8,9,10,11},{16,17,18,19},{24,25,26,27},{32,40,48,56},{33,41,..., dimensions={0} | all-to-all | bytes 4718592 | tf_op jit(solution)/shard_map/cond/branch_8_fun/cond/branch_1_fun/all_to_all | solution.py:234
  54.7 0.0 collective-permute-done.25
  54.7 7.5 %collective-permute-done.26 = bf16[384,384]{1,0:T(8,128)(2,1)} collective-permute-done((bf16[384,384]{1,0:T(8,128)(2,1)}, bf16[384,384]{1,0:T(8,128)(2,1)}, u32[]{:S(2)}, u32[]{:S(2)}) %collective-permute-start.26) | collective-permute-done | bytes 294944 | tf_op jit(solution)/shard_map/cond/branch_8_fun/ppermute | solution.py:281
  62.1 4.4 %collective-permute-start.27 = (bf16[3072,384]{1,0:T(8,128)(2,1)}, bf16[3072,384]{1,0:T(8,128)(2,1)S(1)}, u32[]{:S(2)}, u32[]{:S(2)}) collective-permute-start(bf16[3072,384]{1,0:T(8,128)(2,1)} %get-tuple-element.167.piece_hbm), channel_id=1, source_target_pairs={{0,32},{32,0},{1,33},{33,1},{2,34},{34,2},{3,35},{35,3},{4,36},{36... | collective-permute-start | bytes 7077896 | tf_op jit(solution)/shard_map/ppermute | solution.py:297
  66.5 4.6 %shard_map.73 = (bf16[16,192,384]{2,1,0:T(8,128)(2,1)S(1)}, bf16[256,4608]{1,0:T(8,128)(2,1)S(1)}, bf16[384,384]{1,0:T(8,128)(2,1)S(1)}, bf16[384,384]{1,0:T(8,128)(2,1)S(1)}) custom-call(s32[1]{0:T(128)} %bitcast.49.core_ref, bf16[3072,384]{1,0:T(8,128)(2,1)} %get-tuple-element.167.piece_hbm, bf16[384,384]{1,0:T(8,128)(2,1)} %get-tuple-element.168.fwd_hbm, ...), custom_call_target="tpu_custom_call" | custom-call | flops 1000 | bytes 1000 | tf_op jit(solution)/shard_map/pallas_call | solution.py:171
  71.2 0.0 collective-permute-done.27.piece_ref
  71.2 2.7 %shard_map.74 = (bf16[16,192,384]{2,1,0:T(8,128)(2,1)S(1)}, bf16[256,4608]{1,0:T(8,128)(2,1)S(1)}) custom-call(bf16[3072,384]{1,0:T(8,128)(2,1)S(1)} %collective-permute-done.27.piece_ref, bf16[384,384]{1,0:T(8,128)(2,1)S(1)} %get-tuple-element.171.fwd_ref), custom_call_target="tpu_custom_call" | custom-call | flops 1000 | bytes 1000 | tf_op jit(solution)/shard_map/pallas_call | solution.py:188
  73.9 0.0 copy-start.2
  73.9 0.0 copy-start.1
  73.9 5.2 %shard_map.75 = f32[16,2,16]{2,1,0:T(2,128)} custom-call(bf16[16,192,384]{2,1,0:T(8,128)(2,1)S(1)} %get-tuple-element.170.coef_mine_ref, bf16[16,192,384]{2,1,0:T(8,128)(2,1)S(1)} %get-tuple-element.172.coef_other_ref, bf16[256,4608]{1,0:T(8,128)(2,1)S(1)} %get-tuple-element.173.left_mine_ref, bf16[256,4608]{1,0:T(8,128)(2,1)S(1)} %get-tuple-element.174.left_other_ref, ...), custom_call_target="tpu_custom_call" | custom-call | flops 1000 | bytes 1000 | tf_op jit(solution)/shard_map/pallas_call | solution.py:200
  79.2 8.9 %all-to-all-start.18 = ((f32[16,2,16]{2,1,0:T(2,128)}), f32[16,2,16]{2,1,0:T(2,128)S(1)}, u32[]{:S(2)}, u32[]{:S(2)}) async-start(f32[16,2,16]{2,1,0:T(2,128)} %shard_map.75), calls=%async_computation.18 | async-start | bytes 32768 | tf_op jit(solution)/shard_map/all_to_all | solution.py:306
  88.1 0.0 copy-done.2
  88.1 0.6 dynamic_slice.6
  90.0 0.1 copy.17
  90.1 0.1 copy.19
  90.8 0.2 dynamic-slice_reduce_fusion
  91.0 8.4 %all-to-all-done.18 = f32[16,2,16]{2,1,0:T(2,128)S(1)} async-done(((f32[16,2,16]{2,1,0:T(2,128)}), f32[16,2,16]{2,1,0:T(2,128)S(1)}, u32[]{:S(2)}, u32[]{:S(2)}) %all-to-all-start.18) | async-done | bytes 2080 | tf_op jit(solution)/shard_map/all_to_all | solution.py:306
  99.4 0.6 broadcast_in_dim.117
  100.0 5.1 %all-to-all-start.19 = ((f32[32,1,16]{2,1,0:T(1,128)}), f32[32,1,16]{2,1,0:T(1,128)S(1)}, u32[]{:S(2)}, u32[]{:S(2)}) async-start(f32[32,1,16]{2,1,0:T(1,128)} %bitcast.54), calls=%async_computation.19 | async-start | bytes 32768 | tf_op jit(solution)/shard_map/all_to_all | solution.py:310
  105.2 0.1 multiply_reduce_fusion
  105.3 6.6 %all-to-all-done.19 = f32[32,1,16]{2,1,0:T(1,128)S(1)} async-done(((f32[32,1,16]{2,1,0:T(1,128)}), f32[32,1,16]{2,1,0:T(1,128)S(1)}, u32[]{:S(2)}, u32[]{:S(2)}) %all-to-all-start.19) | async-done | bytes 2080 | tf_op jit(solution)/shard_map/all_to_all | solution.py:310
  111.8 0.1 copy.20
  111.9 0.7 multiply_reduce_fusion.1
  (6 shorter events, 0.1 us)
Async XLA Ops:
  0.0 90.8 %copy-start = (f32[2,128,32]{1,2,0:T(8,128)S(1)}, f32[2,128,32]{1,2,0:T(8,128)}, u32[]{:S(2)}) copy-start(f32[2,128,32]{1,2,0:T(8,128)} %param.38) | copy-start | bytes 98308
  0.7 21.4 %collective-permute-start.24 = (bf16[192,384]{1,0:T(8,128)(2,1)}, bf16[192,384]{1,0:T(8,128)(2,1)S(1)}, u32[]{:S(2)}, u32[]{:S(2)}) collective-permute-start(bf16[192,384]{1,0:T(8,128)(2,1)} %bitcast.109), channel_id=1, source_target_pairs={{0,0},{4,32},{32,4},{36,36},{1,1},{5,33},{33,5},{37,37},{2,2},{6,3... | collective-permute-start | bytes 442376 | tf_op jit(solution)/shard_map/cond/branch_8_fun/ppermute | solution.py:279
  17.6 37.1 %collective-permute-start.25 = (bf16[384,384]{1,0:T(8,128)(2,1)}, bf16[384,384]{1,0:T(8,128)(2,1)}, u32[]{:S(2)}, u32[]{:S(2)}) collective-permute-start(bf16[384,384]{1,0:T(8,128)(2,1)} %get-tuple-element.147), channel_id=1, source_target_pairs={{0,0},{4,32},{32,4},{36,36},{1,1},{5,33},{33,5},{37,37},{2,2},{6,3... | collective-permute-start | bytes 884744 | tf_op jit(solution)/shard_map/cond/branch_8_fun/ppermute | solution.py:280
  19.5 42.6 %collective-permute-start.26 = (bf16[384,384]{1,0:T(8,128)(2,1)}, bf16[384,384]{1,0:T(8,128)(2,1)}, u32[]{:S(2)}, u32[]{:S(2)}) collective-permute-start(bf16[384,384]{1,0:T(8,128)(2,1)} %get-tuple-element.148), channel_id=1, source_target_pairs={{160,0},{164,32},{192,4},{196,36},{224,64},{228,96},{128,68},{132,... | collective-permute-start | bytes 884744 | tf_op jit(solution)/shard_map/cond/branch_8_fun/ppermute | solution.py:281
  62.1 9.0 %collective-permute-start.27 = (bf16[3072,384]{1,0:T(8,128)(2,1)}, bf16[3072,384]{1,0:T(8,128)(2,1)S(1)}, u32[]{:S(2)}, u32[]{:S(2)}) collective-permute-start(bf16[3072,384]{1,0:T(8,128)(2,1)} %get-tuple-element.167.piece_hbm), channel_id=1, source_target_pairs={{0,32},{32,0},{1,33},{33,1},{2,34},{34,2},{3,35},{35,3},{4,36},{36... | collective-permute-start | bytes 7077896 | tf_op jit(solution)/shard_map/ppermute | solution.py:297
  73.9 14.2 %copy-start.2 = (s32[32]{0:T(128)S(1)}, s32[32]{0:T(128)}, u32[]{:S(2)}) copy-start(s32[32]{0:T(128)} %param.40) | copy-start | bytes 388
  73.9 16.1 %copy-start.1 = (f32[32,32]{1,0:T(8,128)S(1)}, f32[32,32]{1,0:T(8,128)}, u32[]{:S(2)}) copy-start(f32[32,32]{1,0:T(8,128)} %param.39) | copy-start | bytes 12292
  79.2 20.2 %all-to-all-start.18 = ((f32[16,2,16]{2,1,0:T(2,128)}), f32[16,2,16]{2,1,0:T(2,128)S(1)}, u32[]{:S(2)}, u32[]{:S(2)}) async-start(f32[16,2,16]{2,1,0:T(2,128)} %shard_map.75), calls=%async_computation.18 | async-start | bytes 32768 | tf_op jit(solution)/shard_map/all_to_all | solution.py:306
  100.0 11.8 %all-to-all-start.19 = ((f32[32,1,16]{2,1,0:T(1,128)}), f32[32,1,16]{2,1,0:T(1,128)S(1)}, u32[]{:S(2)}, u32[]{:S(2)}) async-start(f32[32,1,16]{2,1,0:T(1,128)} %bitcast.54), calls=%async_computation.19 | async-start | bytes 32768 | tf_op jit(solution)/shard_map/all_to_all | solution.py:310

commit v4 on v3

--- a/solution.py
+++ b/solution.py
@@ -37,9 +37,7 @@
     rest = at - side * (size // 2)
     shard = (rest * 171) >> 11
     row = rest - shard * ROWS
-    outer, inner = shard >> 2, shard & 3
-    y = jnp.where(here == 1, outer, inner)
-    x = jnp.where(here == 1, inner, outer)
+    y, x = shard >> 2, shard & 3
     return onehot(((y * 2 + here) * SIDE + x) * ROWS + row, lax.broadcasted_iota(jnp.int32, (size, size), 1))
 
 
@@ -227,23 +225,10 @@
     )(block)
 
 
-def spread(block, phases):
-    for groups in phases:
-        count = len(groups[0])
-        copies = jnp.broadcast_to(block[None], (count,) + block.shape)
-        block = lax.all_to_all(
-            copies, ("c", "y", "x"), 0, 0, axis_index_groups=groups, tiled=True
-        ).reshape(count * block.shape[0], block.shape[1])
-    return block
-
-
-def spread_phases(cores, ys, xs):
-    def index(c, y, x):
-        return (c * ys + y) * xs + x
-
-    along_y = [[[index(c, y, x) for y in range(ys)] for x in range(xs)] for c in range(cores)]
-    along_x = [[[index(c, y, x) for x in range(xs)] for y in range(ys)] for c in range(cores)]
-    return along_y[0] + along_x[1], along_x[0] + along_y[1]
+def spread(block, axes, count):
+    copies = jnp.broadcast_to(block[None], (count,) + block.shape)
+    rows = lax.all_to_all(copies, axes, 0, 0, tiled=True)
+    return rows.reshape(count * block.shape[0], block.shape[1])
 
 
 def shards(sizes, bcoef, fwd_green, back_green, kmq, ir_table, ir_fit, freq_index):
@@ -263,7 +248,6 @@
     minor_shift = ((own_k & 3) - (target & 3)) & 3
     branch = (major_shift - 1) * (minor - 1) + minor_shift - 1
 
-    phases = spread_phases(cores, ys, xs)
     swapped = [(c * zh + h, h * zh + c) for c in range(cores) for h in range(zh)]
 
     def partner(major, minor_by):
@@ -281,7 +265,7 @@
             green_back = lax.ppermute(green_back, ("zl", "c", "zh"), route)
             mine = lax.cond(
                 target >= 0,
-                lambda block: spread(block, phases),
+                lambda block: spread(block, ("y", "x"), ys * xs),
                 lambda block: jnp.zeros((ys * xs * block.shape[0], block.shape[1]), block.dtype),
                 settled(shard),
             )

time: 113 us -> 114 us (level); the launches traced: 113 us -> 115 us
  starting transfers between devices: 39.1 us -> 52.7 us
  waiting for transfers between devices: 22.5 us -> 15 us
  blocking collectives: 32.2 us -> 28.6 us
    all_to_all x1, starting transfers between devices: 8.9 us -> 17.9 us  [shards(): parts = lax.all_to_all(pairs, ('zl', 'zh'), 0, 0, tiled=True)]
    ppermute x1, waiting for transfers between devices: 7.48 us -> 0.01 us  [work(): green_back = lax.ppermute(green_back, ('zl', 'c', 'zh'), route)]
    ppermute x1, starting transfers between devices: 1.92 us -> 8.93 us  [work(): green_back = lax.ppermute(green_back, ('zl', 'c', 'zh'), route)]
    all_to_all x2 -> x1, blocking collectives: 32.2 us -> 28.6 us  [spread(): rows = lax.all_to_all(copies, axes, 0, 0, tiled=True)]
    ppermute x1, starting transfers between devices: 4.38 us -> 2.1 us  [shards(): other = lax.ppermute(mine, 'c', [(0, 1), (1, 0)])]
  transfers between devices with their start and end apart: 6 -> 6, of which waited for: 3 -> 2; matrix products, arithmetic and copies ran while one was open for 1% -> 1% of each run, Pallas kernels for 4% -> 4%
where the time goes in v4:
time: 114 us; the launch traced here: 115 us
  starting transfers between devices  52.7 us (46%)
  blocking collectives  28.6 us (25%)
  waiting for transfers between devices  15 us (13%)
  Pallas kernels  12.6 us (11%)
  between operations  2.72 us (2%)
  local copies, waits for them, and re-layouts  1.88 us (2%)
    all_to_all x1, blocking collectives, spread(): rows = lax.all_to_all(copies, axes, 0, 0, tiled=True)  28.6 us
    all_to_all x1, starting transfers between devices, shards(): parts = lax.all_to_all(pairs, ('zl', 'zh'), 0, 0, tiled=True)  17.9 us
    ppermute x1, starting transfers between devices, work(): shard = lax.ppermute(shard, ('c', 'zh'), swapped)  16.8 us
    ppermute x1, starting transfers between devices, work(): green_back = lax.ppermute(green_back, ('zl', 'c', 'zh'), route)  8.93 us
    all_to_all x1, waiting for transfers between devices, shards(): parts = lax.all_to_all(pairs, ('zl', 'zh'), 0, 0, tiled=True)  8.42 us
    all_to_all x1, waiting for transfers between devices, shards(): times = lax.all_to_all(entries, ('c', 'y', 'x'), 0, 0, tiled=True)  6.57 us
    pallas_call x1, Pallas kernels, product(): pl.pallas_call(product_kernel, out_shape=jax.ShapeDtypeStruct((receivers,...  5.24 us
    all_to_all x1, starting transfers between devices, shards(): times = lax.all_to_all(entries, ('c', 'y', 'x'), 0, 0, tiled=True)  5.06 us
  transfers between devices with their start and end apart: 6, of which 2 were waited for; matrix products, arithmetic and copies ran while one was open for 1% of the time, Pallas kernels for 4%

profile of v4, /device:TPU:1, one launch (start us, length us, event | category | flops | bytes accessed | tf_op | source)
XLA Modules:
  0.0 115.1 jit_solution(7690564843653201420)
XLA Ops:
  0.0 0.0 copy-start
  0.7 57.4 %conditional.10 = (bf16[3072,384]{1,0:T(8,128)(2,1)}, bf16[384,384]{1,0:T(8,128)(2,1)}, bf16[384,384]{1,0:T(8,128)(2,1)}) conditional(s32[]{:T(128)} %clamp.3, (s32[]{:T(128)}, bf16[16,12,384]{2,0,1:T(8,128)(2,1)}, bf16[384,384]{1,0:T(8,128)(2,1)}, bf16[384,384]{1,0:T(8,128)(2,1)}) %tuple.145, (s32[]{:T(128)}, ...), branch_computations={%region_0.0_spmd, %region_3.0_spmd, %region_6.0_spmd, %region_9.0_... | conditional | flops 49999998976 | bytes 12674630 | solution.py:277
  0.7 16.8 %collective-permute-start.12 = (bf16[192,384]{1,0:T(8,128)(2,1)}, bf16[192,384]{1,0:T(8,128)(2,1)S(1)}, u32[]{:S(2)}, u32[]{:S(2)}) collective-permute-start(bf16[192,384]{1,0:T(8,128)(2,1)} %bitcast.87), channel_id=1, source_target_pairs={{0,0},{4,32},{32,4},{36,36},{1,1},{5,33},{33,5},{37,37},{2,2},{6,3... | collective-permute-start | bytes 442376 | tf_op jit(solution)/shard_map/cond/branch_4_fun/ppermute | solution.py:263
  17.5 1.9 %collective-permute-start.13 = (bf16[384,384]{1,0:T(8,128)(2,1)}, bf16[384,384]{1,0:T(8,128)(2,1)}, u32[]{:S(2)}, u32[]{:S(2)}) collective-permute-start(bf16[384,384]{1,0:T(8,128)(2,1)} %get-tuple-element.131), channel_id=1, source_target_pairs={{0,0},{4,32},{32,4},{36,36},{1,1},{5,33},{33,5},{37,37},{2,2},{6,3... | collective-permute-start | bytes 884744 | tf_op jit(solution)/shard_map/cond/branch_4_fun/ppermute | solution.py:264
  19.5 8.9 %collective-permute-start.14 = (bf16[384,384]{1,0:T(8,128)(2,1)}, bf16[384,384]{1,0:T(8,128)(2,1)}, u32[]{:S(2)}, u32[]{:S(2)}) collective-permute-start(bf16[384,384]{1,0:T(8,128)(2,1)} %get-tuple-element.132), channel_id=1, source_target_pairs={{320,0},{324,32},{352,4},{356,36},{256,64},{260,96},{288,68},{292,... | collective-permute-start | bytes 884744 | tf_op jit(solution)/shard_map/cond/branch_4_fun/ppermute | solution.py:265
  29.1 0.0 collective-permute-done.12.block_ref
  29.1 29.0 %conditional.4 = (bf16[3072,384]{1,0:T(8,128)(2,1)}) conditional(s32[]{:T(128)} %convert_element_type.24, () %tuple.76, bf16[192,384]{1,0:T(8,128)(2,1)S(1)} %branch_4_fun.1), branch_computations={%region_13.0_spmd, %region_14.0_spmd} | conditional | bytes 7225352 | solution.py:266
  29.1 0.3 broadcast_in_dim.32
  29.4 28.6 %all_to_all.54 = bf16[16,192,384]{2,1,0:T(8,128)(2,1)} all-to-all(bf16[16,192,384]{2,1,0:T(8,128)(2,1)S(1)} %broadcast_in_dim.32), channel_id=1, replica_groups=mesh['zl'=8,'c'=2,'y'=4,'zh'=2,'x'=4] {'y','x'}, dimensions={0} | all-to-all | bytes 4718592 | tf_op jit(solution)/shard_map/cond/branch_4_fun/cond/branch_1_fun/all_to_all | solution.py:230
  58.1 0.0 collective-permute-done.13
  58.1 0.0 collective-permute-done.14
  58.1 2.1 %collective-permute-start.27 = (bf16[3072,384]{1,0:T(8,128)(2,1)}, bf16[3072,384]{1,0:T(8,128)(2,1)S(1)}, u32[]{:S(2)}, u32[]{:S(2)}) collective-permute-start(bf16[3072,384]{1,0:T(8,128)(2,1)} %get-tuple-element.167.piece_hbm), channel_id=1, source_target_pairs={{0,32},{32,0},{1,33},{33,1},{2,34},{34,2},{3,35},{35,3},{4,36},{36... | collective-permute-start | bytes 7077896 | tf_op jit(solution)/shard_map/ppermute | solution.py:281
  60.2 4.6 %shard_map.73 = (bf16[16,192,384]{2,1,0:T(8,128)(2,1)S(1)}, bf16[256,4608]{1,0:T(8,128)(2,1)S(1)}, bf16[384,384]{1,0:T(8,128)(2,1)S(1)}, bf16[384,384]{1,0:T(8,128)(2,1)S(1)}) custom-call(s32[1]{0:T(128)} %bitcast.40.core_ref, bf16[3072,384]{1,0:T(8,128)(2,1)} %get-tuple-element.167.piece_hbm, bf16[384,384]{1,0:T(8,128)(2,1)} %get-tuple-element.168.fwd_hbm, ...), custom_call_target="tpu_custom_call" | custom-call | flops 1000 | bytes 1000 | tf_op jit(solution)/shard_map/pallas_call | solution.py:169
  64.8 0.0 collective-permute-done.27.piece_ref
  64.8 2.7 %shard_map.74 = (bf16[16,192,384]{2,1,0:T(8,128)(2,1)S(1)}, bf16[256,4608]{1,0:T(8,128)(2,1)S(1)}) custom-call(bf16[3072,384]{1,0:T(8,128)(2,1)S(1)} %collective-permute-done.27.piece_ref, bf16[384,384]{1,0:T(8,128)(2,1)S(1)} %get-tuple-element.171.fwd_ref), custom_call_target="tpu_custom_call" | custom-call | flops 1000 | bytes 1000 | tf_op jit(solution)/shard_map/pallas_call | solution.py:186
  67.5 0.0 copy-start.2
  67.5 0.0 copy-start.1
  67.6 5.2 %shard_map.75 = f32[16,2,16]{2,1,0:T(2,128)} custom-call(bf16[16,192,384]{2,1,0:T(8,128)(2,1)S(1)} %get-tuple-element.170.coef_mine_ref, bf16[16,192,384]{2,1,0:T(8,128)(2,1)S(1)} %get-tuple-element.172.coef_other_ref, bf16[256,4608]{1,0:T(8,128)(2,1)S(1)} %get-tuple-element.173.left_mine_ref, bf16[256,4608]{1,0:T(8,128)(2,1)S(1)} %get-tuple-element.174.left_other_ref, ...), custom_call_target="tpu_custom_call" | custom-call | flops 1000 | bytes 1000 | tf_op jit(solution)/shard_map/pallas_call | solution.py:198
  72.8 17.9 %all-to-all-start.9 = ((f32[16,2,16]{2,1,0:T(2,128)}), f32[16,2,16]{2,1,0:T(2,128)S(1)}, u32[]{:S(2)}, u32[]{:S(2)}) async-start(f32[16,2,16]{2,1,0:T(2,128)} %shard_map.75), calls=%async_computation.9 | async-start | bytes 32768 | tf_op jit(solution)/shard_map/all_to_all | solution.py:290
  90.7 0.0 copy-done.2
  90.7 0.6 dynamic_slice.6
  92.6 0.1 copy.17
  92.7 0.1 copy.19
  93.4 0.0 copy-done
  93.4 0.2 dynamic-slice_reduce_fusion
  93.6 8.4 %all-to-all-done.9 = f32[16,2,16]{2,1,0:T(2,128)S(1)} async-done(((f32[16,2,16]{2,1,0:T(2,128)}), f32[16,2,16]{2,1,0:T(2,128)S(1)}, u32[]{:S(2)}, u32[]{:S(2)}) %all-to-all-start.9) | async-done | bytes 2080 | tf_op jit(solution)/shard_map/all_to_all | solution.py:290
  102.0 0.6 broadcast_in_dim.49
  102.6 5.1 %all-to-all-start.10 = ((f32[32,1,16]{2,1,0:T(1,128)}), f32[32,1,16]{2,1,0:T(1,128)S(1)}, u32[]{:S(2)}, u32[]{:S(2)}) async-start(f32[32,1,16]{2,1,0:T(1,128)} %bitcast.45), calls=%async_computation.10 | async-start | bytes 32768 | tf_op jit(solution)/shard_map/all_to_all | solution.py:294
  107.7 0.1 multiply_reduce_fusion
  107.8 6.6 %all-to-all-done.10 = f32[32,1,16]{2,1,0:T(1,128)S(1)} async-done(((f32[32,1,16]{2,1,0:T(1,128)}), f32[32,1,16]{2,1,0:T(1,128)S(1)}, u32[]{:S(2)}, u32[]{:S(2)}) %all-to-all-start.10) | async-done | bytes 2080 | tf_op jit(solution)/shard_map/all_to_all | solution.py:294
  114.4 0.1 copy.20
  114.4 0.7 multiply_reduce_fusion.1
  (4 shorter events, 0.0 us)
Async XLA Ops:
  0.0 93.4 %copy-start = (f32[2,128,32]{1,2,0:T(8,128)S(1)}, f32[2,128,32]{1,2,0:T(8,128)}, u32[]{:S(2)}) copy-start(f32[2,128,32]{1,2,0:T(8,128)} %param.38) | copy-start | bytes 98308
  0.7 28.4 %collective-permute-start.12 = (bf16[192,384]{1,0:T(8,128)(2,1)}, bf16[192,384]{1,0:T(8,128)(2,1)S(1)}, u32[]{:S(2)}, u32[]{:S(2)}) collective-permute-start(bf16[192,384]{1,0:T(8,128)(2,1)} %bitcast.87), channel_id=1, source_target_pairs={{0,0},{4,32},{32,4},{36,36},{1,1},{5,33},{33,5},{37,37},{2,2},{6,3... | collective-permute-start | bytes 442376 | tf_op jit(solution)/shard_map/cond/branch_4_fun/ppermute | solution.py:263
  17.5 40.5 %collective-permute-start.13 = (bf16[384,384]{1,0:T(8,128)(2,1)}, bf16[384,384]{1,0:T(8,128)(2,1)}, u32[]{:S(2)}, u32[]{:S(2)}) collective-permute-start(bf16[384,384]{1,0:T(8,128)(2,1)} %get-tuple-element.131), channel_id=1, source_target_pairs={{0,0},{4,32},{32,4},{36,36},{1,1},{5,33},{33,5},{37,37},{2,2},{6,3... | collective-permute-start | bytes 884744 | tf_op jit(solution)/shard_map/cond/branch_4_fun/ppermute | solution.py:264
  19.5 38.6 %collective-permute-start.14 = (bf16[384,384]{1,0:T(8,128)(2,1)}, bf16[384,384]{1,0:T(8,128)(2,1)}, u32[]{:S(2)}, u32[]{:S(2)}) collective-permute-start(bf16[384,384]{1,0:T(8,128)(2,1)} %get-tuple-element.132), channel_id=1, source_target_pairs={{320,0},{324,32},{352,4},{356,36},{256,64},{260,96},{288,68},{292,... | collective-permute-start | bytes 884744 | tf_op jit(solution)/shard_map/cond/branch_4_fun/ppermute | solution.py:265
  58.1 6.7 %collective-permute-start.27 = (bf16[3072,384]{1,0:T(8,128)(2,1)}, bf16[3072,384]{1,0:T(8,128)(2,1)S(1)}, u32[]{:S(2)}, u32[]{:S(2)}) collective-permute-start(bf16[3072,384]{1,0:T(8,128)(2,1)} %get-tuple-element.167.piece_hbm), channel_id=1, source_target_pairs={{0,32},{32,0},{1,33},{33,1},{2,34},{34,2},{3,35},{35,3},{4,36},{36... | collective-permute-start | bytes 7077896 | tf_op jit(solution)/shard_map/ppermute | solution.py:281
  67.5 23.2 %copy-start.2 = (s32[32]{0:T(128)S(1)}, s32[32]{0:T(128)}, u32[]{:S(2)}) copy-start(s32[32]{0:T(128)} %param.40) | copy-start | bytes 388
  67.5 25.0 %copy-start.1 = (f32[32,32]{1,0:T(8,128)S(1)}, f32[32,32]{1,0:T(8,128)}, u32[]{:S(2)}) copy-start(f32[32,32]{1,0:T(8,128)} %param.39) | copy-start | bytes 12292
  72.8 29.2 %all-to-all-start.9 = ((f32[16,2,16]{2,1,0:T(2,128)}), f32[16,2,16]{2,1,0:T(2,128)S(1)}, u32[]{:S(2)}, u32[]{:S(2)}) async-start(f32[16,2,16]{2,1,0:T(2,128)} %shard_map.75), calls=%async_computation.9 | async-start | bytes 32768 | tf_op jit(solution)/shard_map/all_to_all | solution.py:290
  102.6 11.7 %all-to-all-start.10 = ((f32[32,1,16]{2,1,0:T(1,128)}), f32[32,1,16]{2,1,0:T(1,128)S(1)}, u32[]{:S(2)}, u32[]{:S(2)}) async-start(f32[32,1,16]{2,1,0:T(1,128)} %bitcast.45), calls=%async_computation.10 | async-start | bytes 32768 | tf_op jit(solution)/shard_map/all_to_all | solution.py:294

commit v5 on v4

--- a/solution.py
+++ b/solution.py
@@ -261,20 +261,20 @@
         def work(shard, green_fwd, green_back):
             shard = shard.transpose(1, 0, 2).reshape(rows * blocks, orb)
             shard = lax.ppermute(shard, ("c", "zh"), swapped)
+            green_back = lax.ppermute(green_back, ("zl", "c", "zh"), route)
             green_fwd = lax.ppermute(green_fwd, ("c", "zh"), swapped)
-            green_back = lax.ppermute(green_back, ("zl", "c", "zh"), route)
             mine = lax.cond(
                 target >= 0,
                 lambda block: spread(block, ("y", "x"), ys * xs),
                 lambda block: jnp.zeros((ys * xs * block.shape[0], block.shape[1]), block.dtype),
                 settled(shard),
             )
-            return mine, green_fwd, green_back
+            return mine, green_back, green_fwd
 
         return work
 
     works = [partner(a, b) for a in range(1, SIDE) for b in range(1, minor)]
-    mine, green_fwd, green_back = lax.switch(
+    mine, green_back, green_fwd = lax.switch(
         branch, works, bcoef[0], fwd_green[0, 0], back_green[0, 0]
     )
     mine, own_w, core = lax.optimization_barrier((mine, own_w.astype(jnp.uint32), core))

time: 114 us -> 112 us (0.982); the launches traced: 115 us -> 111 us
  starting transfers between devices: 52.7 us -> 39.6 us
  blocking collectives: 28.6 us -> 38.1 us
    all_to_all x1, blocking collectives: 28.6 us -> 38.1 us  [spread(): rows = lax.all_to_all(copies, axes, 0, 0, tiled=True)]
    all_to_all x1, starting transfers between devices: 17.9 us -> 9.86 us  [shards(): parts = lax.all_to_all(pairs, ('zl', 'zh'), 0, 0, tiled=True)]
    ppermute x1, starting transfers between devices: 8.93 us -> 1.92 us  [work(): green_back = lax.ppermute(green_back, ('zl', 'c', 'zh'), route)]
    ppermute x1, starting transfers between devices: 1.92 us -> 3.36 us  [work(): green_fwd = lax.ppermute(green_fwd, ('c', 'zh'), swapped)]
where the time goes in v5:
time: 112 us; the launch traced here: 111 us
  starting transfers between devices  39.6 us (35%)
  blocking collectives  38.1 us (34%)
  waiting for transfers between devices  15 us (13%)
  Pallas kernels  12.6 us (11%)
  between operations  2.72 us (2%)
  local copies, waits for them, and re-layouts  1.88 us (2%)
    all_to_all x1, blocking collectives, spread(): rows = lax.all_to_all(copies, axes, 0, 0, tiled=True)  38.1 us
    ppermute x1, starting transfers between devices, work(): shard = lax.ppermute(shard, ('c', 'zh'), swapped)  16.8 us
    all_to_all x1, starting transfers between devices, shards(): parts = lax.all_to_all(pairs, ('zl', 'zh'), 0, 0, tiled=True)  9.86 us
    all_to_all x1, waiting for transfers between devices, shards(): parts = lax.all_to_all(pairs, ('zl', 'zh'), 0, 0, tiled=True)  8.42 us
    all_to_all x1, waiting for transfers between devices, shards(): times = lax.all_to_all(entries, ('c', 'y', 'x'), 0, 0, tiled=True)  6.61 us
    pallas_call x1, Pallas kernels, product(): pl.pallas_call(product_kernel, out_shape=jax.ShapeDtypeStruct((receivers,...  5.24 us
    all_to_all x1, starting transfers between devices, shards(): times = lax.all_to_all(entries, ('c', 'y', 'x'), 0, 0, tiled=True)  5.17 us
    pallas_call x1, Pallas kernels, first_half(): pl.pallas_call(first_kernel, out_shape=half_shapes(piece, blocks) + (squa...  4.61 us
  transfers between devices with their start and end apart: 6, of which 2 were waited for; matrix products, arithmetic and copies ran while one was open for 1% of the time, Pallas kernels for 4%

profile of v5, /device:TPU:1, one launch (start us, length us, event | category | flops | bytes accessed | tf_op | source)
XLA Modules:
  0.0 111.5 jit_solution(3356230096191350444)
XLA Ops:
  0.0 0.0 copy-start
  0.7 61.3 %conditional.10 = (bf16[3072,384]{1,0:T(8,128)(2,1)}, bf16[384,384]{1,0:T(8,128)(2,1)}, bf16[384,384]{1,0:T(8,128)(2,1)}) conditional(s32[]{:T(128)} %clamp.3, (s32[]{:T(128)}, bf16[16,12,384]{2,0,1:T(8,128)(2,1)}, bf16[384,384]{1,0:T(8,128)(2,1)}, bf16[384,384]{1,0:T(8,128)(2,1)}) %tuple.145, (s32[]{:T(128)}, ...), branch_computations={%region_0.0_spmd, %region_3.0_spmd, %region_6.0_spmd, %region_9.0_... | conditional | flops 49999998976 | bytes 12674630 | solution.py:277
  0.7 16.8 %collective-permute-start.9 = (bf16[192,384]{1,0:T(8,128)(2,1)}, bf16[192,384]{1,0:T(8,128)(2,1)S(1)}, u32[]{:S(2)}, u32[]{:S(2)}) collective-permute-start(bf16[192,384]{1,0:T(8,128)(2,1)} %bitcast.86), channel_id=1, source_target_pairs={{0,0},{4,32},{32,4},{36,36},{1,1},{5,33},{33,5},{37,37},{2,2},{6,3... | collective-permute-start | bytes 442376 | tf_op jit(solution)/shard_map/cond/branch_3_fun/ppermute | solution.py:263
  17.5 1.9 %collective-permute-start.10 = (bf16[384,384]{1,0:T(8,128)(2,1)}, bf16[384,384]{1,0:T(8,128)(2,1)}, u32[]{:S(2)}, u32[]{:S(2)}) collective-permute-start(bf16[384,384]{1,0:T(8,128)(2,1)} %get-tuple-element.127), channel_id=1, source_target_pairs={{352,0},{356,32},{256,4},{260,36},{288,64},{292,96},{320,68},{324,... | collective-permute-start | bytes 884744 | tf_op jit(solution)/shard_map/cond/branch_3_fun/ppermute | solution.py:264
  19.5 3.4 %collective-permute-start.11 = (bf16[384,384]{1,0:T(8,128)(2,1)}, bf16[384,384]{1,0:T(8,128)(2,1)}, u32[]{:S(2)}, u32[]{:S(2)}) collective-permute-start(bf16[384,384]{1,0:T(8,128)(2,1)} %get-tuple-element.128), channel_id=1, source_target_pairs={{0,0},{4,32},{32,4},{36,36},{1,1},{5,33},{33,5},{37,37},{2,2},{6,3... | collective-permute-start | bytes 884744 | tf_op jit(solution)/shard_map/cond/branch_3_fun/ppermute | solution.py:265
  23.5 0.0 collective-permute-done.9.block_ref
  23.5 38.4 %conditional.3 = (bf16[3072,384]{1,0:T(8,128)(2,1)}) conditional(s32[]{:T(128)} %convert_element_type.23, () %tuple.74, bf16[192,384]{1,0:T(8,128)(2,1)S(1)} %branch_3_fun.1), branch_computations={%region_10.0_spmd, %region_11.0_spmd} | conditional | bytes 7225352 | solution.py:266
  23.6 0.3 broadcast_in_dim.27
  23.9 38.1 %all_to_all.53 = bf16[16,192,384]{2,1,0:T(8,128)(2,1)} all-to-all(bf16[16,192,384]{2,1,0:T(8,128)(2,1)S(1)} %broadcast_in_dim.27), channel_id=1, replica_groups=mesh['zl'=8,'c'=2,'y'=4,'zh'=2,'x'=4] {'y','x'}, dimensions={0} | all-to-all | bytes 4718592 | tf_op jit(solution)/shard_map/cond/branch_3_fun/cond/branch_1_fun/all_to_all | solution.py:230
  61.9 0.0 collective-permute-done.10
  61.9 0.0 collective-permute-done.11
  61.9 2.5 %collective-permute-start.27 = (bf16[3072,384]{1,0:T(8,128)(2,1)}, bf16[3072,384]{1,0:T(8,128)(2,1)S(1)}, u32[]{:S(2)}, u32[]{:S(2)}) collective-permute-start(bf16[3072,384]{1,0:T(8,128)(2,1)} %get-tuple-element.167.piece_hbm), channel_id=1, source_target_pairs={{0,32},{32,0},{1,33},{33,1},{2,34},{34,2},{3,35},{35,3},{4,36},{36... | collective-permute-start | bytes 7077896 | tf_op jit(solution)/shard_map/ppermute | solution.py:281
  64.4 4.6 %shard_map.73 = (bf16[16,192,384]{2,1,0:T(8,128)(2,1)S(1)}, bf16[256,4608]{1,0:T(8,128)(2,1)S(1)}, bf16[384,384]{1,0:T(8,128)(2,1)S(1)}, bf16[384,384]{1,0:T(8,128)(2,1)S(1)}) custom-call(s32[1]{0:T(128)} %bitcast.40.core_ref, bf16[3072,384]{1,0:T(8,128)(2,1)} %get-tuple-element.167.piece_hbm, bf16[384,384]{1,0:T(8,128)(2,1)} %get-tuple-element.168.fwd_hbm, ...), custom_call_target="tpu_custom_call" | custom-call | flops 1000 | bytes 1000 | tf_op jit(solution)/shard_map/pallas_call | solution.py:169
  69.0 0.0 collective-permute-done.27.piece_ref
  69.1 2.7 %shard_map.74 = (bf16[16,192,384]{2,1,0:T(8,128)(2,1)S(1)}, bf16[256,4608]{1,0:T(8,128)(2,1)S(1)}) custom-call(bf16[3072,384]{1,0:T(8,128)(2,1)S(1)} %collective-permute-done.27.piece_ref, bf16[384,384]{1,0:T(8,128)(2,1)S(1)} %get-tuple-element.171.fwd_ref), custom_call_target="tpu_custom_call" | custom-call | flops 1000 | bytes 1000 | tf_op jit(solution)/shard_map/pallas_call | solution.py:186
  71.8 0.0 copy-start.2
  71.8 0.0 copy-start.1
  71.8 5.2 %shard_map.75 = f32[16,2,16]{2,1,0:T(2,128)} custom-call(bf16[16,192,384]{2,1,0:T(8,128)(2,1)S(1)} %get-tuple-element.170.coef_mine_ref, bf16[16,192,384]{2,1,0:T(8,128)(2,1)S(1)} %get-tuple-element.172.coef_other_ref, bf16[256,4608]{1,0:T(8,128)(2,1)S(1)} %get-tuple-element.173.left_mine_ref, bf16[256,4608]{1,0:T(8,128)(2,1)S(1)} %get-tuple-element.174.left_other_ref, ...), custom_call_target="tpu_custom_call" | custom-call | flops 1000 | bytes 1000 | tf_op jit(solution)/shard_map/pallas_call | solution.py:198
  77.0 9.9 %all-to-all-start.9 = ((f32[16,2,16]{2,1,0:T(2,128)}), f32[16,2,16]{2,1,0:T(2,128)S(1)}, u32[]{:S(2)}, u32[]{:S(2)}) async-start(f32[16,2,16]{2,1,0:T(2,128)} %shard_map.75), calls=%async_computation.9 | async-start | bytes 32768 | tf_op jit(solution)/shard_map/all_to_all | solution.py:290
  86.9 0.0 copy-done.2
  86.9 0.6 dynamic_slice.6
  88.8 0.0 copy-done.1
  88.8 0.1 copy.17
  88.9 0.1 copy.19
  89.7 0.2 dynamic-slice_reduce_fusion
  89.8 8.4 %all-to-all-done.9 = f32[16,2,16]{2,1,0:T(2,128)S(1)} async-done(((f32[16,2,16]{2,1,0:T(2,128)}), f32[16,2,16]{2,1,0:T(2,128)S(1)}, u32[]{:S(2)}, u32[]{:S(2)}) %all-to-all-start.9) | async-done | bytes 2080 | tf_op jit(solution)/shard_map/all_to_all | solution.py:290
  98.3 0.6 broadcast_in_dim.49
  98.9 5.2 %all-to-all-start.10 = ((f32[32,1,16]{2,1,0:T(1,128)}), f32[32,1,16]{2,1,0:T(1,128)S(1)}, u32[]{:S(2)}, u32[]{:S(2)}) async-start(f32[32,1,16]{2,1,0:T(1,128)} %bitcast.45), calls=%async_computation.10 | async-start | bytes 32768 | tf_op jit(solution)/shard_map/all_to_all | solution.py:294
  104.0 0.1 multiply_reduce_fusion
  104.1 6.6 %all-to-all-done.10 = f32[32,1,16]{2,1,0:T(1,128)S(1)} async-done(((f32[32,1,16]{2,1,0:T(1,128)}), f32[32,1,16]{2,1,0:T(1,128)S(1)}, u32[]{:S(2)}, u32[]{:S(2)}) %all-to-all-start.10) | async-done | bytes 2080 | tf_op jit(solution)/shard_map/all_to_all | solution.py:294
  110.7 0.1 copy.20
  110.8 0.7 multiply_reduce_fusion.1
  (4 shorter events, 0.1 us)
Async XLA Ops:
  0.0 89.6 %copy-start = (f32[2,128,32]{1,2,0:T(8,128)S(1)}, f32[2,128,32]{1,2,0:T(8,128)}, u32[]{:S(2)}) copy-start(f32[2,128,32]{1,2,0:T(8,128)} %param.38) | copy-start | bytes 98308
  0.7 22.8 %collective-permute-start.9 = (bf16[192,384]{1,0:T(8,128)(2,1)}, bf16[192,384]{1,0:T(8,128)(2,1)S(1)}, u32[]{:S(2)}, u32[]{:S(2)}) collective-permute-start(bf16[192,384]{1,0:T(8,128)(2,1)} %bitcast.86), channel_id=1, source_target_pairs={{0,0},{4,32},{32,4},{36,36},{1,1},{5,33},{33,5},{37,37},{2,2},{6,3... | collective-permute-start | bytes 442376 | tf_op jit(solution)/shard_map/cond/branch_3_fun/ppermute | solution.py:263
  17.5 44.4 %collective-permute-start.10 = (bf16[384,384]{1,0:T(8,128)(2,1)}, bf16[384,384]{1,0:T(8,128)(2,1)}, u32[]{:S(2)}, u32[]{:S(2)}) collective-permute-start(bf16[384,384]{1,0:T(8,128)(2,1)} %get-tuple-element.127), channel_id=1, source_target_pairs={{352,0},{356,32},{256,4},{260,36},{288,64},{292,96},{320,68},{324,... | collective-permute-start | bytes 884744 | tf_op jit(solution)/shard_map/cond/branch_3_fun/ppermute | solution.py:264
  19.5 42.5 %collective-permute-start.11 = (bf16[384,384]{1,0:T(8,128)(2,1)}, bf16[384,384]{1,0:T(8,128)(2,1)}, u32[]{:S(2)}, u32[]{:S(2)}) collective-permute-start(bf16[384,384]{1,0:T(8,128)(2,1)} %get-tuple-element.128), channel_id=1, source_target_pairs={{0,0},{4,32},{32,4},{36,36},{1,1},{5,33},{33,5},{37,37},{2,2},{6,3... | collective-permute-start | bytes 884744 | tf_op jit(solution)/shard_map/cond/branch_3_fun/ppermute | solution.py:265
  61.9 7.1 %collective-permute-start.27 = (bf16[3072,384]{1,0:T(8,128)(2,1)}, bf16[3072,384]{1,0:T(8,128)(2,1)S(1)}, u32[]{:S(2)}, u32[]{:S(2)}) collective-permute-start(bf16[3072,384]{1,0:T(8,128)(2,1)} %get-tuple-element.167.piece_hbm), channel_id=1, source_target_pairs={{0,32},{32,0},{1,33},{33,1},{2,34},{34,2},{3,35},{35,3},{4,36},{36... | collective-permute-start | bytes 7077896 | tf_op jit(solution)/shard_map/ppermute | solution.py:281
  71.8 15.1 %copy-start.2 = (s32[32]{0:T(128)S(1)}, s32[32]{0:T(128)}, u32[]{:S(2)}) copy-start(s32[32]{0:T(128)} %param.40) | copy-start | bytes 388
  71.8 17.0 %copy-start.1 = (f32[32,32]{1,0:T(8,128)S(1)}, f32[32,32]{1,0:T(8,128)}, u32[]{:S(2)}) copy-start(f32[32,32]{1,0:T(8,128)} %param.39) | copy-start | bytes 12292
  77.0 21.2 %all-to-all-start.9 = ((f32[16,2,16]{2,1,0:T(2,128)}), f32[16,2,16]{2,1,0:T(2,128)S(1)}, u32[]{:S(2)}, u32[]{:S(2)}) async-start(f32[16,2,16]{2,1,0:T(2,128)} %shard_map.75), calls=%async_computation.9 | async-start | bytes 32768 | tf_op jit(solution)/shard_map/all_to_all | solution.py:290
  98.9 11.9 %all-to-all-start.10 = ((f32[32,1,16]{2,1,0:T(1,128)}), f32[32,1,16]{2,1,0:T(1,128)S(1)}, u32[]{:S(2)}, u32[]{:S(2)}) async-start(f32[32,1,16]{2,1,0:T(1,128)} %bitcast.45), calls=%async_computation.10 | async-start | bytes 32768 | tf_op jit(solution)/shard_map/all_to_all | solution.py:294

commit v6 on v4

--- a/solution.py
+++ b/solution.py
@@ -14,7 +14,7 @@
 TILE = 16
 POINTS = 16
 FIRST_LIMIT = 10 * 1024 * 1024
-PRODUCT_LIMIT = 14 * 1024 * 1024
+PRODUCT_LIMIT = 20 * 1024 * 1024
 SMALL_LIMIT = 8 * 1024 * 1024
 COST = pl.CostEstimate(flops=1000, bytes_accessed=1000, transcendentals=0)
 
@@ -101,19 +101,16 @@
     back_t_ref[...] = back_t.astype(jnp.bfloat16)
 
 
-def left_kernel(piece_ref, fwd_ref, coef_ref, left_ref):
-    order = swap_order(coef_ref.shape[0])
-    step = STEP
-
-    @pl.loop(0, coef_ref.shape[1] // TILE // step)
-    def _(turn):
-        left_turn(order, piece_ref, fwd_ref, coef_ref, left_ref, turn, step)
-
-
 def product_kernel(
-    coef_mine_ref, coef_other_ref, left_mine_ref, left_other_ref, back_t_ref, out_ref, right_ref
+    coef_mine_ref, left_mine_ref, piece_ref, fwd_ref, back_t_ref, out_ref, coef_other_ref, left_other_ref, right_ref
 ):
     blocks, half, width = coef_mine_ref.shape
+    order = swap_order(blocks)
+
+    @pl.loop(0, half // TILE // STEP)
+    def _(turn):
+        left_turn(order, piece_ref, fwd_ref, coef_other_ref, left_other_ref, turn, STEP)
+
     per_side = half // TILE
 
     @pl.loop(0, blocks // 2, unroll=4)
@@ -182,18 +179,7 @@
     )(core, piece, green_fwd, green_back)
 
 
-def second_half(piece, green_fwd, blocks):
-    return pl.pallas_call(
-        left_kernel,
-        out_shape=half_shapes(piece, blocks),
-        in_specs=[pl.BlockSpec(memory_space=pltpu.VMEM)] * 2,
-        out_specs=[pl.BlockSpec(memory_space=pltpu.VMEM)] * 2,
-        compiler_params=pltpu.CompilerParams(vmem_limit_bytes=SMALL_LIMIT),
-        cost_estimate=COST,
-    )(piece, green_fwd)
-
-
-def product(coef_mine, coef_other, left_mine, left_other, back_t, receivers, cores):
+def product(coef_mine, left_mine, other, green_fwd, back_t, receivers, cores):
     blocks, half, width = coef_mine.shape
     return pl.pallas_call(
         product_kernel,
@@ -201,11 +187,13 @@
         in_specs=[pl.BlockSpec(memory_space=pltpu.VMEM)] * 5,
         out_specs=pl.BlockSpec(memory_space=pltpu.VMEM),
         scratch_shapes=[
+            pltpu.VMEM(coef_mine.shape, jnp.bfloat16),
+            pltpu.VMEM(left_mine.shape, jnp.bfloat16),
             pltpu.VMEM((2, blocks * TILE, half // TILE * width), jnp.bfloat16),
         ],
         compiler_params=pltpu.CompilerParams(vmem_limit_bytes=PRODUCT_LIMIT),
         cost_estimate=COST,
-    )(coef_mine, coef_other, left_mine, left_other, back_t)
+    )(coef_mine, left_mine, other, green_fwd, back_t)
 
 
 def settle_kernel(block_ref, out_ref):
@@ -282,8 +270,7 @@
     coef_mine, left_mine, green_fwd, back_t = first_half(
         core[None], mine, green_fwd, green_back, blocks
     )
-    coef_other, left_other = second_half(other, green_fwd, blocks)
-    pairs = product(coef_mine, coef_other, left_mine, left_other, back_t, zl * zh, cores)
+    pairs = product(coef_mine, left_mine, other, green_fwd, back_t, zl * zh, cores)
     pairs, ir_table, ir_fit, freq_index = lax.optimization_barrier(
         (pairs, ir_table, ir_fit, freq_index)
     )

time: 114 us -> 113 us (level); the launches traced: 115 us -> 112 us
  starting transfers between devices: 52.7 us -> 48 us
  blocking collectives: 28.6 us -> 30.4 us
    ppermute x1, starting transfers between devices: 2.1 us -> 10.9 us  [shards(): other = lax.ppermute(mine, 'c', [(0, 1), (1, 0)])]
    ppermute x1, starting transfers between devices: 8.93 us -> 1.92 us  [work(): green_back = lax.ppermute(green_back, ('zl', 'c', 'zh'), route)]
    all_to_all x1, starting transfers between devices: 17.9 us -> 11.3 us  [shards(): parts = lax.all_to_all(pairs, ('zl', 'zh'), 0, 0, tiled=True)]
    pallas_call x1 -> x0, Pallas kernels: 2.72 us -> none  [second_half(): pl.pallas_call(left_kernel, out_shape=half_shapes(piece, blocks), in_spec...]
    pallas_call x1, Pallas kernels: 5.24 us -> 7.91 us  [product(): pl.pallas_call(product_kernel, out_shape=jax.ShapeDtypeStruct((receivers,...]
    all_to_all x1, blocking collectives: 28.6 us -> 30.4 us  [spread(): rows = lax.all_to_all(copies, axes, 0, 0, tiled=True)]
where the time goes in v6:
time: 113 us; the launch traced here: 112 us
  starting transfers between devices  48 us (42%)
  blocking collectives  30.4 us (27%)
  waiting for transfers between devices  15.2 us (13%)
  Pallas kernels  12.5 us (11%)
  between operations  2.72 us (2%)
  local copies, waits for them, and re-layouts  1.88 us (2%)
    all_to_all x1, blocking collectives, spread(): rows = lax.all_to_all(copies, axes, 0, 0, tiled=True)  30.4 us
    ppermute x1, starting transfers between devices, work(): shard = lax.ppermute(shard, ('c', 'zh'), swapped)  16.8 us
    all_to_all x1, starting transfers between devices, shards(): parts = lax.all_to_all(pairs, ('zl', 'zh'), 0, 0, tiled=True)  11.3 us
    ppermute x1, starting transfers between devices, shards(): other = lax.ppermute(mine, 'c', [(0, 1), (1, 0)])  10.9 us
    all_to_all x1, waiting for transfers between devices, shards(): parts = lax.all_to_all(pairs, ('zl', 'zh'), 0, 0, tiled=True)  8.42 us
    pallas_call x1, Pallas kernels, product(): pl.pallas_call(product_kernel, out_shape=jax.ShapeDtypeStruct((receivers,...  7.91 us
    all_to_all x1, waiting for transfers between devices, shards(): times = lax.all_to_all(entries, ('c', 'y', 'x'), 0, 0, tiled=True)  6.73 us
    all_to_all x1, starting transfers between devices, shards(): times = lax.all_to_all(entries, ('c', 'y', 'x'), 0, 0, tiled=True)  5.09 us
  transfers between devices with their start and end apart: 6, of which 2 were waited for; matrix products, arithmetic and copies ran while one was open for 1% of the time, Pallas kernels for 4%

profile of v6, /device:TPU:1, one launch (start us, length us, event | category | flops | bytes accessed | tf_op | source)
XLA Modules:
  0.0 112.1 jit_solution(5124688934530886885)
XLA Ops:
  0.0 0.0 copy-start
  0.7 52.1 %conditional.10 = (bf16[3072,384]{1,0:T(8,128)(2,1)}, bf16[384,384]{1,0:T(8,128)(2,1)}, bf16[384,384]{1,0:T(8,128)(2,1)}) conditional(s32[]{:T(128)} %clamp.3, (s32[]{:T(128)}, bf16[16,12,384]{2,0,1:T(8,128)(2,1)}, bf16[384,384]{1,0:T(8,128)(2,1)}, bf16[384,384]{1,0:T(8,128)(2,1)}) %tuple.145, (s32[]{:T(128)}, ...), branch_computations={%region_0.0_spmd, %region_3.0_spmd, %region_6.0_spmd, %region_9.0_... | conditional | flops 49999998976 | bytes 12674630 | solution.py:265
  0.7 16.8 %collective-permute-start.15 = (bf16[192,384]{1,0:T(8,128)(2,1)}, bf16[192,384]{1,0:T(8,128)(2,1)S(1)}, u32[]{:S(2)}, u32[]{:S(2)}) collective-permute-start(bf16[192,384]{1,0:T(8,128)(2,1)} %bitcast.88), channel_id=1, source_target_pairs={{0,0},{4,32},{32,4},{36,36},{1,1},{5,33},{33,5},{37,37},{2,2},{6,3... | collective-permute-start | bytes 442376 | tf_op jit(solution)/shard_map/cond/branch_5_fun/ppermute | solution.py:251
  17.6 1.9 %collective-permute-start.16 = (bf16[384,384]{1,0:T(8,128)(2,1)}, bf16[384,384]{1,0:T(8,128)(2,1)}, u32[]{:S(2)}, u32[]{:S(2)}) collective-permute-start(bf16[384,384]{1,0:T(8,128)(2,1)} %get-tuple-element.135), channel_id=1, source_target_pairs={{0,0},{4,32},{32,4},{36,36},{1,1},{5,33},{33,5},{37,37},{2,2},{6,3... | collective-permute-start | bytes 884744 | tf_op jit(solution)/shard_map/cond/branch_5_fun/ppermute | solution.py:252
  19.5 1.9 %collective-permute-start.17 = (bf16[384,384]{1,0:T(8,128)(2,1)}, bf16[384,384]{1,0:T(8,128)(2,1)}, u32[]{:S(2)}, u32[]{:S(2)}) collective-permute-start(bf16[384,384]{1,0:T(8,128)(2,1)} %get-tuple-element.136), channel_id=1, source_target_pairs={{288,0},{292,32},{320,4},{324,36},{352,64},{356,96},{256,68},{260,... | collective-permute-start | bytes 884744 | tf_op jit(solution)/shard_map/cond/branch_5_fun/ppermute | solution.py:253
  22.1 0.0 collective-permute-done.15.block_ref
  22.1 30.7 %conditional.5 = (bf16[3072,384]{1,0:T(8,128)(2,1)}) conditional(s32[]{:T(128)} %convert_element_type.25, () %tuple.78, bf16[192,384]{1,0:T(8,128)(2,1)S(1)} %branch_5_fun.1), branch_computations={%region_16.0_spmd, %region_17.0_spmd} | conditional | bytes 7225352 | solution.py:254
  22.1 0.3 broadcast_in_dim.33
  22.4 30.4 %all_to_all.55 = bf16[16,192,384]{2,1,0:T(8,128)(2,1)} all-to-all(bf16[16,192,384]{2,1,0:T(8,128)(2,1)S(1)} %broadcast_in_dim.33), channel_id=1, replica_groups=mesh['zl'=8,'c'=2,'y'=4,'zh'=2,'x'=4] {'y','x'}, dimensions={0} | all-to-all | bytes 4718592 | tf_op jit(solution)/shard_map/cond/branch_5_fun/cond/branch_1_fun/all_to_all | solution.py:218
  52.8 0.0 collective-permute-done.16
  52.8 0.0 collective-permute-done.17
  52.8 10.9 %collective-permute-start.27 = (bf16[3072,384]{1,0:T(8,128)(2,1)}, bf16[3072,384]{1,0:T(8,128)(2,1)S(1)}, u32[]{:S(2)}, u32[]{:S(2)}) collective-permute-start(bf16[3072,384]{1,0:T(8,128)(2,1)} %get-tuple-element.165.piece_hbm), channel_id=1, source_target_pairs={{0,32},{32,0},{1,33},{33,1},{2,34},{34,2},{3,35},{35,3},{4,36},{36... | collective-permute-start | bytes 7077896 | tf_op jit(solution)/shard_map/ppermute | solution.py:269
  63.6 4.6 %shard_map.73 = (bf16[16,192,384]{2,1,0:T(8,128)(2,1)S(1)}, bf16[256,4608]{1,0:T(8,128)(2,1)S(1)}, bf16[384,384]{1,0:T(8,128)(2,1)S(1)}, bf16[384,384]{1,0:T(8,128)(2,1)S(1)}) custom-call(s32[1]{0:T(128)} %bitcast.40.core_ref, bf16[3072,384]{1,0:T(8,128)(2,1)} %get-tuple-element.165.piece_hbm, bf16[384,384]{1,0:T(8,128)(2,1)} %get-tuple-element.166.fwd_hbm, ...), custom_call_target="tpu_custom_call" | custom-call | flops 1000 | bytes 1000 | tf_op jit(solution)/shard_map/pallas_call | solution.py:166
  68.3 0.0 collective-permute-done.27.piece_ref
  68.3 0.0 copy-start.2
  68.3 0.0 copy-start.1
  68.3 7.9 %shard_map.74 = f32[16,2,16]{2,1,0:T(2,128)} custom-call(bf16[16,192,384]{2,1,0:T(8,128)(2,1)S(1)} %get-tuple-element.168.coef_mine_ref, bf16[256,4608]{1,0:T(8,128)(2,1)S(1)} %get-tuple-element.169.left_mine_ref, bf16[3072,384]{1,0:T(8,128)(2,1)S(1)} %collective-permute-done.27.piece_ref, bf16[384,384]{1,0:T(8,128)(2,1)S(1)} %get-tuple-element.170.fwd_ref, ...), custom_call_target="tpu_custom_call" | custom-call | flops 1000 | bytes 1000 | tf_op jit(solution)/shard_map/pallas_call | solution.py:184
  76.2 11.3 %all-to-all-start.9 = ((f32[16,2,16]{2,1,0:T(2,128)}), f32[16,2,16]{2,1,0:T(2,128)S(1)}, u32[]{:S(2)}, u32[]{:S(2)}) async-start(f32[16,2,16]{2,1,0:T(2,128)} %shard_map.74), calls=%async_computation.9 | async-start | bytes 32768 | tf_op jit(solution)/shard_map/all_to_all | solution.py:277
  87.5 0.0 copy-done.2
  87.6 0.6 dynamic_slice.6
  89.4 0.0 copy-done.1
  89.4 0.1 copy.17
  89.5 0.1 copy.19
  90.3 0.0 copy-done
  90.3 0.2 dynamic-slice_reduce_fusion
  90.4 8.4 %all-to-all-done.9 = f32[16,2,16]{2,1,0:T(2,128)S(1)} async-done(((f32[16,2,16]{2,1,0:T(2,128)}), f32[16,2,16]{2,1,0:T(2,128)S(1)}, u32[]{:S(2)}, u32[]{:S(2)}) %all-to-all-start.9) | async-done | bytes 2080 | tf_op jit(solution)/shard_map/all_to_all | solution.py:277
  98.9 0.6 broadcast_in_dim.49
  99.5 5.1 %all-to-all-start.10 = ((f32[32,1,16]{2,1,0:T(1,128)}), f32[32,1,16]{2,1,0:T(1,128)S(1)}, u32[]{:S(2)}, u32[]{:S(2)}) async-start(f32[32,1,16]{2,1,0:T(1,128)} %bitcast.45), calls=%async_computation.10 | async-start | bytes 32768 | tf_op jit(solution)/shard_map/all_to_all | solution.py:281
  104.6 0.1 multiply_reduce_fusion
  104.7 6.7 %all-to-all-done.10 = f32[32,1,16]{2,1,0:T(1,128)S(1)} async-done(((f32[32,1,16]{2,1,0:T(1,128)}), f32[32,1,16]{2,1,0:T(1,128)S(1)}, u32[]{:S(2)}, u32[]{:S(2)}) %all-to-all-start.10) | async-done | bytes 2080 | tf_op jit(solution)/shard_map/all_to_all | solution.py:281
  111.4 0.1 copy.20
  111.5 0.7 multiply_reduce_fusion.1
  (3 shorter events, 0.0 us)
Async XLA Ops:
  0.0 90.3 %copy-start = (f32[2,128,32]{1,2,0:T(8,128)S(1)}, f32[2,128,32]{1,2,0:T(8,128)}, u32[]{:S(2)}) copy-start(f32[2,128,32]{1,2,0:T(8,128)} %param.38) | copy-start | bytes 98308
  0.7 21.4 %collective-permute-start.15 = (bf16[192,384]{1,0:T(8,128)(2,1)}, bf16[192,384]{1,0:T(8,128)(2,1)S(1)}, u32[]{:S(2)}, u32[]{:S(2)}) collective-permute-start(bf16[192,384]{1,0:T(8,128)(2,1)} %bitcast.88), channel_id=1, source_target_pairs={{0,0},{4,32},{32,4},{36,36},{1,1},{5,33},{33,5},{37,37},{2,2},{6,3... | collective-permute-start | bytes 442376 | tf_op jit(solution)/shard_map/cond/branch_5_fun/ppermute | solution.py:251
  17.6 35.2 %collective-permute-start.16 = (bf16[384,384]{1,0:T(8,128)(2,1)}, bf16[384,384]{1,0:T(8,128)(2,1)}, u32[]{:S(2)}, u32[]{:S(2)}) collective-permute-start(bf16[384,384]{1,0:T(8,128)(2,1)} %get-tuple-element.135), channel_id=1, source_target_pairs={{0,0},{4,32},{32,4},{36,36},{1,1},{5,33},{33,5},{37,37},{2,2},{6,3... | collective-permute-start | bytes 884744 | tf_op jit(solution)/shard_map/cond/branch_5_fun/ppermute | solution.py:252
  19.5 33.3 %collective-permute-start.17 = (bf16[384,384]{1,0:T(8,128)(2,1)}, bf16[384,384]{1,0:T(8,128)(2,1)}, u32[]{:S(2)}, u32[]{:S(2)}) collective-permute-start(bf16[384,384]{1,0:T(8,128)(2,1)} %get-tuple-element.136), channel_id=1, source_target_pairs={{288,0},{292,32},{320,4},{324,36},{352,64},{356,96},{256,68},{260,... | collective-permute-start | bytes 884744 | tf_op jit(solution)/shard_map/cond/branch_5_fun/ppermute | solution.py:253
  52.8 15.5 %collective-permute-start.27 = (bf16[3072,384]{1,0:T(8,128)(2,1)}, bf16[3072,384]{1,0:T(8,128)(2,1)S(1)}, u32[]{:S(2)}, u32[]{:S(2)}) collective-permute-start(bf16[3072,384]{1,0:T(8,128)(2,1)} %get-tuple-element.165.piece_hbm), channel_id=1, source_target_pairs={{0,32},{32,0},{1,33},{33,1},{2,34},{34,2},{3,35},{35,3},{4,36},{36... | collective-permute-start | bytes 7077896 | tf_op jit(solution)/shard_map/ppermute | solution.py:269
  68.3 19.3 %copy-start.2 = (s32[32]{0:T(128)S(1)}, s32[32]{0:T(128)}, u32[]{:S(2)}) copy-start(s32[32]{0:T(128)} %param.40) | copy-start | bytes 388
  68.3 21.2 %copy-start.1 = (f32[32,32]{1,0:T(8,128)S(1)}, f32[32,32]{1,0:T(8,128)}, u32[]{:S(2)}) copy-start(f32[32,32]{1,0:T(8,128)} %param.39) | copy-start | bytes 12292
  76.2 22.7 %all-to-all-start.9 = ((f32[16,2,16]{2,1,0:T(2,128)}), f32[16,2,16]{2,1,0:T(2,128)S(1)}, u32[]{:S(2)}, u32[]{:S(2)}) async-start(f32[16,2,16]{2,1,0:T(2,128)} %shard_map.74), calls=%async_computation.9 | async-start | bytes 32768 | tf_op jit(solution)/shard_map/all_to_all | solution.py:277
  99.5 11.9 %all-to-all-start.10 = ((f32[32,1,16]{2,1,0:T(1,128)}), f32[32,1,16]{2,1,0:T(1,128)S(1)}, u32[]{:S(2)}, u32[]{:S(2)}) async-start(f32[32,1,16]{2,1,0:T(1,128)} %bitcast.45), calls=%async_computation.10 | async-start | bytes 32768 | tf_op jit(solution)/shard_map/all_to_all | solution.py:281

commit v7 on v6

--- a/solution.py
+++ b/solution.py
@@ -107,9 +107,9 @@
     blocks, half, width = coef_mine_ref.shape
     order = swap_order(blocks)
 
-    @pl.loop(0, half // TILE // STEP)
+    @pl.loop(0, half // TILE // (STEP + 2))
     def _(turn):
-        left_turn(order, piece_ref, fwd_ref, coef_other_ref, left_other_ref, turn, STEP)
+        left_turn(order, piece_ref, fwd_ref, coef_other_ref, left_other_ref, turn, STEP + 2)
 
     per_side = half // TILE
 

time: 113 us -> 112 us (level); the launches traced: 112 us -> 113 us
  blocking collectives: 30.4 us -> 32.2 us
  starting transfers between devices: 48 us -> 46.8 us
    ppermute x1, starting transfers between devices: 10.9 us -> 2.1 us  [shards(): other = lax.ppermute(mine, 'c', [(0, 1), (1, 0)])]
    ppermute x1, starting transfers between devices: 1.92 us -> 8.04 us  [work(): green_back = lax.ppermute(green_back, ('zl', 'c', 'zh'), route)]
    all_to_all x1, blocking collectives: 30.4 us -> 32.2 us  [spread(): rows = lax.all_to_all(copies, axes, 0, 0, tiled=True)]
    all_to_all x1, starting transfers between devices: 11.3 us -> 12.8 us  [shards(): parts = lax.all_to_all(pairs, ('zl', 'zh'), 0, 0, tiled=True)]
where the time goes in v7:
time: 112 us; the launch traced here: 113 us
  starting transfers between devices  46.8 us (42%)
  blocking collectives  32.2 us (29%)
  waiting for transfers between devices  15.2 us (14%)
  Pallas kernels  12.4 us (11%)
  between operations  2.72 us (2%)
  local copies, waits for them, and re-layouts  1.88 us (2%)
    all_to_all x1, blocking collectives, spread(): rows = lax.all_to_all(copies, axes, 0, 0, tiled=True)  32.2 us
    ppermute x1, starting transfers between devices, work(): shard = lax.ppermute(shard, ('c', 'zh'), swapped)  16.8 us
    all_to_all x1, starting transfers between devices, shards(): parts = lax.all_to_all(pairs, ('zl', 'zh'), 0, 0, tiled=True)  12.8 us
    all_to_all x1, waiting for transfers between devices, shards(): parts = lax.all_to_all(pairs, ('zl', 'zh'), 0, 0, tiled=True)  8.42 us
    ppermute x1, starting transfers between devices, work(): green_back = lax.ppermute(green_back, ('zl', 'c', 'zh'), route)  8.04 us
    pallas_call x1, Pallas kernels, product(): pl.pallas_call(product_kernel, out_shape=jax.ShapeDtypeStruct((receivers,...  7.78 us
    all_to_all x1, waiting for transfers between devices, shards(): times = lax.all_to_all(entries, ('c', 'y', 'x'), 0, 0, tiled=True)  6.73 us
    all_to_all x1, starting transfers between devices, shards(): times = lax.all_to_all(entries, ('c', 'y', 'x'), 0, 0, tiled=True)  5.09 us
  transfers between devices with their start and end apart: 6, of which 2 were waited for; matrix products, arithmetic and copies ran while one was open for 1% of the time, Pallas kernels for 4%

profile of v7, /device:TPU:1, one launch (start us, length us, event | category | flops | bytes accessed | tf_op | source)
XLA Modules:
  0.0 112.7 jit_solution(4182108288898829598)
XLA Ops:
  0.0 0.0 copy-start
  0.7 60.1 %conditional.10 = (bf16[3072,384]{1,0:T(8,128)(2,1)}, bf16[384,384]{1,0:T(8,128)(2,1)}, bf16[384,384]{1,0:T(8,128)(2,1)}) conditional(s32[]{:T(128)} %clamp.3, (s32[]{:T(128)}, bf16[16,12,384]{2,0,1:T(8,128)(2,1)}, bf16[384,384]{1,0:T(8,128)(2,1)}, bf16[384,384]{1,0:T(8,128)(2,1)}) %tuple.145, (s32[]{:T(128)}, ...), branch_computations={%region_0.0_spmd, %region_3.0_spmd, %region_6.0_spmd, %region_9.0_... | conditional | flops 49999998976 | bytes 12674630 | solution.py:265
  0.7 16.8 %collective-permute-start.21 = (bf16[192,384]{1,0:T(8,128)(2,1)}, bf16[192,384]{1,0:T(8,128)(2,1)S(1)}, u32[]{:S(2)}, u32[]{:S(2)}) collective-permute-start(bf16[192,384]{1,0:T(8,128)(2,1)} %bitcast.90), channel_id=1, source_target_pairs={{0,0},{4,32},{32,4},{36,36},{1,1},{5,33},{33,5},{37,37},{2,2},{6,3... | collective-permute-start | bytes 442376 | tf_op jit(solution)/shard_map/cond/branch_7_fun/ppermute | solution.py:251
  17.6 1.9 %collective-permute-start.22 = (bf16[384,384]{1,0:T(8,128)(2,1)}, bf16[384,384]{1,0:T(8,128)(2,1)}, u32[]{:S(2)}, u32[]{:S(2)}) collective-permute-start(bf16[384,384]{1,0:T(8,128)(2,1)} %get-tuple-element.143), channel_id=1, source_target_pairs={{0,0},{4,32},{32,4},{36,36},{1,1},{5,33},{33,5},{37,37},{2,2},{6,3... | collective-permute-start | bytes 884744 | tf_op jit(solution)/shard_map/cond/branch_7_fun/ppermute | solution.py:252
  19.5 8.0 %collective-permute-start.23 = (bf16[384,384]{1,0:T(8,128)(2,1)}, bf16[384,384]{1,0:T(8,128)(2,1)}, u32[]{:S(2)}, u32[]{:S(2)}) collective-permute-start(bf16[384,384]{1,0:T(8,128)(2,1)} %get-tuple-element.144), channel_id=1, source_target_pairs={{192,0},{196,32},{224,4},{228,36},{128,64},{132,96},{160,68},{164,... | collective-permute-start | bytes 884744 | tf_op jit(solution)/shard_map/cond/branch_7_fun/ppermute | solution.py:253
  28.2 0.0 collective-permute-done.21.block_ref
  28.2 32.5 %conditional.7 = (bf16[3072,384]{1,0:T(8,128)(2,1)}) conditional(s32[]{:T(128)} %convert_element_type.27, () %tuple.82, bf16[192,384]{1,0:T(8,128)(2,1)S(1)} %branch_7_fun.1), branch_computations={%region_22.0_spmd, %region_23.0_spmd} | conditional | bytes 7225352 | solution.py:254
  28.2 0.3 broadcast_in_dim.35
  28.6 32.2 %all_to_all.57 = bf16[16,192,384]{2,1,0:T(8,128)(2,1)} all-to-all(bf16[16,192,384]{2,1,0:T(8,128)(2,1)S(1)} %broadcast_in_dim.35), channel_id=1, replica_groups=mesh['zl'=8,'c'=2,'y'=4,'zh'=2,'x'=4] {'y','x'}, dimensions={0} | all-to-all | bytes 4718592 | tf_op jit(solution)/shard_map/cond/branch_7_fun/cond/branch_1_fun/all_to_all | solution.py:218
  60.7 0.0 collective-permute-done.22
  60.7 0.0 collective-permute-done.23
  60.8 2.1 %collective-permute-start.27 = (bf16[3072,384]{1,0:T(8,128)(2,1)}, bf16[3072,384]{1,0:T(8,128)(2,1)S(1)}, u32[]{:S(2)}, u32[]{:S(2)}) collective-permute-start(bf16[3072,384]{1,0:T(8,128)(2,1)} %get-tuple-element.165.piece_hbm), channel_id=1, source_target_pairs={{0,32},{32,0},{1,33},{33,1},{2,34},{34,2},{3,35},{35,3},{4,36},{36... | collective-permute-start | bytes 7077896 | tf_op jit(solution)/shard_map/ppermute | solution.py:269
  62.9 4.6 %shard_map.73 = (bf16[16,192,384]{2,1,0:T(8,128)(2,1)S(1)}, bf16[256,4608]{1,0:T(8,128)(2,1)S(1)}, bf16[384,384]{1,0:T(8,128)(2,1)S(1)}, bf16[384,384]{1,0:T(8,128)(2,1)S(1)}) custom-call(s32[1]{0:T(128)} %bitcast.40.core_ref, bf16[3072,384]{1,0:T(8,128)(2,1)} %get-tuple-element.165.piece_hbm, bf16[384,384]{1,0:T(8,128)(2,1)} %get-tuple-element.166.fwd_hbm, ...), custom_call_target="tpu_custom_call" | custom-call | flops 1000 | bytes 1000 | tf_op jit(solution)/shard_map/pallas_call | solution.py:166
  67.5 0.0 collective-permute-done.27.piece_ref
  67.5 0.0 copy-start.2
  67.5 0.0 copy-start.1
  67.5 7.8 %shard_map.74 = f32[16,2,16]{2,1,0:T(2,128)} custom-call(bf16[16,192,384]{2,1,0:T(8,128)(2,1)S(1)} %get-tuple-element.168.coef_mine_ref, bf16[256,4608]{1,0:T(8,128)(2,1)S(1)} %get-tuple-element.169.left_mine_ref, bf16[3072,384]{1,0:T(8,128)(2,1)S(1)} %collective-permute-done.27.piece_ref, bf16[384,384]{1,0:T(8,128)(2,1)S(1)} %get-tuple-element.170.fwd_ref, ...), custom_call_target="tpu_custom_call" | custom-call | flops 1000 | bytes 1000 | tf_op jit(solution)/shard_map/pallas_call | solution.py:184
  75.3 12.8 %all-to-all-start.9 = ((f32[16,2,16]{2,1,0:T(2,128)}), f32[16,2,16]{2,1,0:T(2,128)S(1)}, u32[]{:S(2)}, u32[]{:S(2)}) async-start(f32[16,2,16]{2,1,0:T(2,128)} %shard_map.74), calls=%async_computation.9 | async-start | bytes 32768 | tf_op jit(solution)/shard_map/all_to_all | solution.py:277
  88.1 0.0 copy-done.2
  88.1 0.6 dynamic_slice.6
  90.0 0.0 copy-done.1
  90.0 0.1 copy.17
  90.1 0.1 copy.19
  90.8 0.0 copy-done
  90.8 0.2 dynamic-slice_reduce_fusion
  91.0 8.4 %all-to-all-done.9 = f32[16,2,16]{2,1,0:T(2,128)S(1)} async-done(((f32[16,2,16]{2,1,0:T(2,128)}), f32[16,2,16]{2,1,0:T(2,128)S(1)}, u32[]{:S(2)}, u32[]{:S(2)}) %all-to-all-start.9) | async-done | bytes 2080 | tf_op jit(solution)/shard_map/all_to_all | solution.py:277
  99.4 0.6 broadcast_in_dim.49
  100.0 5.1 %all-to-all-start.10 = ((f32[32,1,16]{2,1,0:T(1,128)}), f32[32,1,16]{2,1,0:T(1,128)S(1)}, u32[]{:S(2)}, u32[]{:S(2)}) async-start(f32[32,1,16]{2,1,0:T(1,128)} %bitcast.45), calls=%async_computation.10 | async-start | bytes 32768 | tf_op jit(solution)/shard_map/all_to_all | solution.py:281
  105.1 0.1 multiply_reduce_fusion
  105.2 6.7 %all-to-all-done.10 = f32[32,1,16]{2,1,0:T(1,128)S(1)} async-done(((f32[32,1,16]{2,1,0:T(1,128)}), f32[32,1,16]{2,1,0:T(1,128)S(1)}, u32[]{:S(2)}, u32[]{:S(2)}) %all-to-all-start.10) | async-done | bytes 2080 | tf_op jit(solution)/shard_map/all_to_all | solution.py:281
  112.0 0.1 copy.20
  112.0 0.7 multiply_reduce_fusion.1
  (3 shorter events, 0.0 us)
Async XLA Ops:
  0.0 90.8 %copy-start = (f32[2,128,32]{1,2,0:T(8,128)S(1)}, f32[2,128,32]{1,2,0:T(8,128)}, u32[]{:S(2)}) copy-start(f32[2,128,32]{1,2,0:T(8,128)} %param.38) | copy-start | bytes 98308
  0.7 27.5 %collective-permute-start.21 = (bf16[192,384]{1,0:T(8,128)(2,1)}, bf16[192,384]{1,0:T(8,128)(2,1)S(1)}, u32[]{:S(2)}, u32[]{:S(2)}) collective-permute-start(bf16[192,384]{1,0:T(8,128)(2,1)} %bitcast.90), channel_id=1, source_target_pairs={{0,0},{4,32},{32,4},{36,36},{1,1},{5,33},{33,5},{37,37},{2,2},{6,3... | collective-permute-start | bytes 442376 | tf_op jit(solution)/shard_map/cond/branch_7_fun/ppermute | solution.py:251
  17.6 43.2 %collective-permute-start.22 = (bf16[384,384]{1,0:T(8,128)(2,1)}, bf16[384,384]{1,0:T(8,128)(2,1)}, u32[]{:S(2)}, u32[]{:S(2)}) collective-permute-start(bf16[384,384]{1,0:T(8,128)(2,1)} %get-tuple-element.143), channel_id=1, source_target_pairs={{0,0},{4,32},{32,4},{36,36},{1,1},{5,33},{33,5},{37,37},{2,2},{6,3... | collective-permute-start | bytes 884744 | tf_op jit(solution)/shard_map/cond/branch_7_fun/ppermute | solution.py:252
  19.5 41.3 %collective-permute-start.23 = (bf16[384,384]{1,0:T(8,128)(2,1)}, bf16[384,384]{1,0:T(8,128)(2,1)}, u32[]{:S(2)}, u32[]{:S(2)}) collective-permute-start(bf16[384,384]{1,0:T(8,128)(2,1)} %get-tuple-element.144), channel_id=1, source_target_pairs={{192,0},{196,32},{224,4},{228,36},{128,64},{132,96},{160,68},{164,... | collective-permute-start | bytes 884744 | tf_op jit(solution)/shard_map/cond/branch_7_fun/ppermute | solution.py:253
  60.8 6.7 %collective-permute-start.27 = (bf16[3072,384]{1,0:T(8,128)(2,1)}, bf16[3072,384]{1,0:T(8,128)(2,1)S(1)}, u32[]{:S(2)}, u32[]{:S(2)}) collective-permute-start(bf16[3072,384]{1,0:T(8,128)(2,1)} %get-tuple-element.165.piece_hbm), channel_id=1, source_target_pairs={{0,32},{32,0},{1,33},{33,1},{2,34},{34,2},{3,35},{35,3},{4,36},{36... | collective-permute-start | bytes 7077896 | tf_op jit(solution)/shard_map/ppermute | solution.py:269
  67.5 20.6 %copy-start.2 = (s32[32]{0:T(128)S(1)}, s32[32]{0:T(128)}, u32[]{:S(2)}) copy-start(s32[32]{0:T(128)} %param.40) | copy-start | bytes 388
  67.5 22.5 %copy-start.1 = (f32[32,32]{1,0:T(8,128)S(1)}, f32[32,32]{1,0:T(8,128)}, u32[]{:S(2)}) copy-start(f32[32,32]{1,0:T(8,128)} %param.39) | copy-start | bytes 12292
  75.3 24.1 %all-to-all-start.9 = ((f32[16,2,16]{2,1,0:T(2,128)}), f32[16,2,16]{2,1,0:T(2,128)S(1)}, u32[]{:S(2)}, u32[]{:S(2)}) async-start(f32[16,2,16]{2,1,0:T(2,128)} %shard_map.74), calls=%async_computation.9 | async-start | bytes 32768 | tf_op jit(solution)/shard_map/all_to_all | solution.py:277
  100.0 11.9 %all-to-all-start.10 = ((f32[32,1,16]{2,1,0:T(1,128)}), f32[32,1,16]{2,1,0:T(1,128)S(1)}, u32[]{:S(2)}, u32[]{:S(2)}) async-start(f32[32,1,16]{2,1,0:T(1,128)} %bitcast.45), calls=%async_computation.10 | async-start | bytes 32768 | tf_op jit(solution)/shard_map/all_to_all | solution.py:281
